TPU v7x, 32 devices: a whole 2x2x4 slice. The times are simulated.
32 devices in a mesh: frame: 8 (over z, x), strip: 4 (over y, core).
Axes of the slice: x: 2, y: 2, z: 4, core: 2. Of those that a mesh axis runs over, the one named last changes fastest.
Arguments:
- features: bfloat16 [8, 120, 32, 256], P('frame', None, 'strip'), may hold values from -6 to 6
- w_mutual: bfloat16 [2, 120, 360], replicated, may hold values from -4 to 4
- w_self: bfloat16 [2, 120, 360], replicated, may hold values from -4 to 4
- w_proj: bfloat16 [2, 240, 120], replicated, may hold values from -0.375 to 0.375
- w_gate: bfloat16 [2, 120, 240], replicated, may hold values from -0.5 to 0.5
- w_up: bfloat16 [2, 120, 240], replicated, may hold values from -0.5 to 0.5
- w_down: bfloat16 [2, 240, 120], replicated, may hold values from -0.375 to 0.375
Outputs:
- refined: bfloat16 [8, 120, 32, 256], P('frame', None, 'strip')
All inputs are finite; a program needn't handle non-finite values.
Results may differ from a plain program's by a relative error of at most 0.012.
The roundings to bfloat16 on the way count: a program that leaves them out, or rounds other values in their place, can miss the bound.
Values may be sent and summed in bfloat16 or wider, within the bound.
A program may use at most 64 MiB of HBM per device.

v0:
```python
import jax
import jax.numpy as jnp
from jax import lax
from jax.sharding import PartitionSpec as P

C = 120
HEADS = 6
HEAD = 20
WIN = 8


epsilon = 1e-05
block_cols = 64


def swapped(block, axis, bit):
    count = lax.axis_size(axis)
    route = []
    for low in range(count):
        high = low | 1 << bit
        if high != low and high < count:
            route += [(low, high), (high, low)]
    return lax.ppermute(block, axis, route)


def from_behind(value, axis, steps):
    count = lax.axis_size(axis)
    pairs = [(source, (source + steps) % count) for source in range(count)]
    return lax.ppermute(value, axis, pairs)


def normed(values):
    centre_mean = jnp.mean(values, axis=0, keepdims=True)
    centred = values - centre_mean
    spread = jnp.mean(centred * centred, axis=0, keepdims=True)
    return (centred * lax.rsqrt(spread + epsilon)).astype(jnp.bfloat16)


def project(weight, values):
    return jnp.einsum("ck,crw->krw", weight, values, preferred_element_type=jnp.float32)


def to_windows(strip_data):
    win_count = strip_data.shape[2] // WIN
    shaped = strip_data.reshape(HEADS, HEAD, WIN, win_count, WIN)
    return shaped.transpose(3, 0, 2, 4, 1).reshape(win_count, HEADS, WIN * WIN, HEAD)


def from_windows(mixed_out):
    win_count = mixed_out.shape[0]
    shaped = mixed_out.reshape(win_count, HEADS, WIN, WIN, HEAD)
    return shaped.transpose(1, 4, 2, 0, 3).reshape(HEADS * HEAD, WIN, win_count * WIN)


def window_mix(queries, key_rows, values):
    scores = jnp.einsum(
        "nhqd,nhkd->nhqk", queries, key_rows, preferred_element_type=jnp.float32
    ) * HEAD ** (-0.5)
    row_max = jnp.max(scores, axis=-1, keepdims=True)
    weights = jnp.exp(scores - row_max)
    weights = (weights / jnp.sum(weights, axis=-1, keepdims=True)).astype(jnp.bfloat16)
    return jnp.einsum(
        "nhqk,nhkd->nhqd", weights, values, preferred_element_type=jnp.float32
    ).astype(jnp.bfloat16)


def attend(own_mut, own_self, other_kv):
    block_count = own_mut.shape[2] // block_cols

    def column_block(position):
        col_start = position * block_cols

        def take_cols(array):
            return lax.dynamic_slice_in_dim(array, col_start, block_cols, 2)

        mutual = window_mix(
            to_windows(take_cols(own_mut[:C])),
            to_windows(take_cols(other_kv[:C])),
            to_windows(take_cols(other_kv[C : 2 * C])),
        )
        key_rows = jnp.concatenate(
            [
                to_windows(take_cols(own_self[C : 2 * C])),
                to_windows(take_cols(other_kv[2 * C : 3 * C])),
            ],
            axis=2,
        )
        value_rows = jnp.concatenate(
            [to_windows(take_cols(own_self[2 * C :])), to_windows(take_cols(other_kv[3 * C :]))],
            axis=2,
        )
        selfish = window_mix(to_windows(take_cols(own_self[:C])), key_rows, value_rows)
        return jnp.concatenate([from_windows(mutual), from_windows(selfish)], axis=0)

    blocks = lax.map(column_block, jnp.arange(block_count, dtype=jnp.int32))
    return blocks.transpose(1, 2, 0, 3).reshape(2 * C, WIN, block_count * block_cols)


def project_all(current, w_mut, w_slf):
    normal_rows = normed(current.astype(jnp.float32))
    return (
        normal_rows,
        project(w_mut, normal_rows).astype(jnp.bfloat16),
        project(w_slf, normal_rows).astype(jnp.bfloat16),
    )


def partner_swap(own_mut, own_self):
    return swapped(jnp.concatenate([own_mut[C:], own_self[C:]], axis=0), "frame", 0)


def finish(current, own_mut, own_self, other_kv, w_prj, w_gte, w_upp, w_dwn):
    joined = attend(own_mut, own_self, other_kv)
    middle = current.astype(jnp.float32) + project(w_prj, joined)
    second_norm = normed(middle)
    hidden = (
        jax.nn.gelu(project(w_gte, second_norm), approximate=False) * project(w_upp, second_norm)
    ).astype(jnp.bfloat16)
    return (middle + project(w_dwn, hidden)).astype(jnp.bfloat16)


def on_device(features, w_mutual, w_self, w_proj, w_gate, w_up, w_down):
    half_win = WIN // 2
    current = features[0]
    norm_one, mut_one, self_one = project_all(current, w_mutual[0], w_self[0])
    partner_one = partner_swap(mut_one, self_one)
    layer_one = finish(
        current, mut_one, self_one, partner_one, w_proj[0], w_gate[0], w_up[0], w_down[0]
    )
    from_below = from_behind(layer_one[:, :half_win], "strip", -1)
    window = jnp.roll(
        jnp.concatenate([layer_one[:, half_win:], from_below], axis=1), -half_win, axis=2
    )
    moved = from_behind(window, "frame", -1)
    norm_two, mut_two, self_two = project_all(moved, w_mutual[1], w_self[1])
    partner_two = partner_swap(mut_two, self_two)
    result_two = finish(
        moved, mut_two, self_two, partner_two, w_proj[1], w_gate[1], w_up[1], w_down[1]
    )
    layer_two = from_behind(result_two, "frame", 1)
    layer_two = jnp.roll(layer_two, half_win, axis=2)
    from_above = from_behind(layer_two[:, half_win:], "strip", 1)
    return jnp.concatenate([from_above, layer_two[:, :half_win]], axis=1)[None]


def solution(mesh):
    in_specs = (P("frame", None, "strip", None), P(), P(), P(), P(), P(), P())
    out_specs = P("frame", None, "strip", None)
    return jax.shard_map(
        on_device, mesh=mesh, in_specs=in_specs, out_specs=out_specs, check_vma=False
    )
```

profile of v0, /device:TPU:0, one launch (start us, length us, event | category | flops | bytes accessed | tf_op | source)
XLA Modules:
  0.0 429.1 jit_solution(16061508467747330020)
XLA Ops:
  6.2 2.9 collective-permute-start
  12.3 40.0 %collective-permute-done = bf16[480,8,256]{2,0,1:T(8,128)(2,1)} collective-permute-done((bf16[480,8,256]{2,0,1:T(8,128)(2,1)}, bf16[480,8,256]{2,0,1:T(8,128)(2,1)}, u32[]{:S(2)}, u32[]{:S(2)}) %collective-permute-start) | collective-permute-done | bytes 1966112 | tf_op jit(solution)/shard_map/ppermute | solution.py:23
  52.3 3.9 copy.78
  57.3 128.6 %while.20 = (s32[]{:T(128)}, bf16[4,240,8,64]{1,3,2,0:T(8,128)(2,1)}, bf16[360,8,256]{0,2,1:T(8,128)(2,1)}, s32[4]{0:T(128)S(1)}, bf16[480,8,256]{0,2,1:T(8,128)...) while((s32[]{:T(128)}, bf16[4,240,8,64]{1,3,2,0:T(8,128)(2,1)}, ...), condition=%wide.region_7.8_spmd, body=%wide.region_2.7_spmd.sunk | while | flops 77003136 | bytes 20193540 | solution.py:95
  60.3 3.9 fusion.409
  67.9 2.5 convolution_convert_fusion.13
  81.0 5.7 %convolution_convert_fusion.12 = bf16[8,6,64,20]{2,3,1,0:T(8,128)(2,1)S(1)} fusion(f32[8,6,64]{2,1,0:T(8,128)S(1)} %fusion.410, bf16[8,6,64,20]{2,3,1,0:T(8,128)(2,1)S(1)} %copy-done.1, bf16[8,6,64,20]{2,3,1,0:T(8,128)(2,1)S(1)} %copy.265, bf16[8,6,8,8,20]{4,1,3,0,2:T(8,128)(2,1)S(1)} %bitcast.558, bf16[8,6,64,20]{2,3,1,0:T(8,128)(2,1)S(1)} %copy-done.3, ...), kind=kOutput, calls=%fused_computation.11.clone.1 | convolution fusion | flops 34077824 | bytes 749568 | tf_op jit(solution)/shard_map/while/body/eval_jaxpr/nhqk,nhkd->nhqd/dot_general | solution.py:62
  92.4 3.9 fusion.409
  99.9 2.5 convolution_convert_fusion.13
  113.0 5.7 %convolution_convert_fusion.12 = bf16[8,6,64,20]{2,3,1,0:T(8,128)(2,1)S(1)} fusion(f32[8,6,64]{2,1,0:T(8,128)S(1)} %fusion.410, bf16[8,6,64,20]{2,3,1,0:T(8,128)(2,1)S(1)} %copy-done.1, bf16[8,6,64,20]{2,3,1,0:T(8,128)(2,1)S(1)} %copy.265, bf16[8,6,8,8,20]{4,1,3,0,2:T(8,128)(2,1)S(1)} %bitcast.558, bf16[8,6,64,20]{2,3,1,0:T(8,128)(2,1)S(1)} %copy-done.3, ...), kind=kOutput, calls=%fused_computation.11.clone.1 | convolution fusion | flops 34077824 | bytes 749568 | tf_op jit(solution)/shard_map/while/body/eval_jaxpr/nhqk,nhkd->nhqd/dot_general | solution.py:62
  124.4 3.9 fusion.409
  145.0 5.7 %convolution_convert_fusion.12 = bf16[8,6,64,20]{2,3,1,0:T(8,128)(2,1)S(1)} fusion(f32[8,6,64]{2,1,0:T(8,128)S(1)} %fusion.410, bf16[8,6,64,20]{2,3,1,0:T(8,128)(2,1)S(1)} %copy-done.1, bf16[8,6,64,20]{2,3,1,0:T(8,128)(2,1)S(1)} %copy.265, bf16[8,6,8,8,20]{4,1,3,0,2:T(8,128)(2,1)S(1)} %bitcast.558, bf16[8,6,64,20]{2,3,1,0:T(8,128)(2,1)S(1)} %copy-done.3, ...), kind=kOutput, calls=%fused_computation.11.clone.1 | convolution fusion | flops 34077824 | bytes 749568 | tf_op jit(solution)/shard_map/while/body/eval_jaxpr/nhqk,nhkd->nhqd/dot_general | solution.py:62
  156.4 3.9 fusion.409
  177.0 5.7 %convolution_convert_fusion.12 = bf16[8,6,64,20]{2,3,1,0:T(8,128)(2,1)S(1)} fusion(f32[8,6,64]{2,1,0:T(8,128)S(1)} %fusion.410, bf16[8,6,64,20]{2,3,1,0:T(8,128)(2,1)S(1)} %copy-done.1, bf16[8,6,64,20]{2,3,1,0:T(8,128)(2,1)S(1)} %copy.265, bf16[8,6,8,8,20]{4,1,3,0,2:T(8,128)(2,1)S(1)} %bitcast.558, bf16[8,6,64,20]{2,3,1,0:T(8,128)(2,1)S(1)} %copy-done.3, ...), kind=kOutput, calls=%fused_computation.11.clone.1 | convolution fusion | flops 34077824 | bytes 749568 | tf_op jit(solution)/shard_map/while/body/eval_jaxpr/nhqk,nhkd->nhqd/dot_general | solution.py:62
  188.6 5.9 %fusion.153 = bf16[120,8,256]{2,0,1:T(8,128)(2,1)S(1)} fusion(f32[120,8,256]{2,0,1:T(8,128)S(1)} %get-tuple-element.142, f32[8,256,240]{1,2,0:T(8,128)S(1)} %fusion.224, f32[8,256]{1,0:T(8,128)S(1)} %add_rsqrt_fusion.2, f32[8,256]{1,0:T(8,128)S(1)} %broadcast_multiply_fusion.2, bf16[2,240,120]{2,1,0:T(8,128)(2,1)} %param.17, bf16[2,120,240]{2,1,0:T(8,128)(2,1)} %param.15), kind=kOutput, calls=%fused_computation.171 | convolution fusion | flops 269598720 | bytes 4562944 | tf_op jit(solution)/shard_map/ck,crw->krw/dot_general | solution.py:40
  194.9 3.7 collective-permute-done.1
  199.1 4.6 %collective-permute-start.2 = (bf16[120,8,256]{2,0,1:T(8,128)(2,1)S(1)}, bf16[120,8,256]{2,0,1:T(8,128)(2,1)S(1)}, u32[]{:S(2)}, u32[]{:S(2)}) collective-permute-start(bf16[120,8,256]{2,0,1:T(8,128)(2,1)S(1)} %fusion.229), channel_id=1, source_target_pairs={{0,28},{4,0},{8,4},{12,8},{16,12},{20,16},{24,20},{28,24},{1,29},{... | collective-permute-start | bytes 1474568 | tf_op jit(solution)/shard_map/ppermute | solution.py:29
  203.7 10.9 %collective-permute-done.2 = bf16[120,8,256]{2,0,1:T(8,128)(2,1)S(1)} collective-permute-done((bf16[120,8,256]{2,0,1:T(8,128)(2,1)S(1)}, bf16[120,8,256]{2,0,1:T(8,128)(2,1)S(1)}, u32[]{:S(2)}, u32[]{:S(2)}) %collective-permute-start.2) | collective-permute-done | bytes 491552 | tf_op jit(solution)/shard_map/ppermute | solution.py:29
  221.3 42.4 %collective-permute-done.3 = bf16[480,8,256]{2,0,1:T(8,128)(2,1)} collective-permute-done((bf16[480,8,256]{2,0,1:T(8,128)(2,1)}, bf16[480,8,256]{2,0,1:T(8,128)(2,1)}, u32[]{:S(2)}, u32[]{:S(2)}) %collective-permute-start.3) | collective-permute-done | bytes 1966112 | tf_op jit(solution)/shard_map/ppermute | solution.py:23
  263.7 3.9 copy.88
  268.7 128.4 %while.21 = (s32[]{:T(128)}, bf16[4,240,8,64]{1,3,2,0:T(8,128)(2,1)}, bf16[360,8,256]{0,2,1:T(8,128)(2,1)}, s32[4]{0:T(128)S(1)}, bf16[480,8,256]{0,2,1:T(8,128)...) while((s32[]{:T(128)}, ...), condition=%wide.region_17.18_spmd, body=%wide.region_12.17_spmd.sunk | while | flops 77003136 | bytes 20193540 | solution.py:95
  271.7 3.9 fusion.424
  292.3 5.7 %convolution_convert_fusion.14 = bf16[8,6,64,20]{2,3,1,0:T(8,128)(2,1)S(1)} fusion(f32[8,6,64]{2,1,0:T(8,128)S(1)} %fusion.425, bf16[8,6,64,20]{2,3,1,0:T(8,128)(2,1)S(1)} %copy-done.2, bf16[8,6,64,20]{2,3,1,0:T(8,128)(2,1)S(1)} %copy.284, bf16[8,6,8,8,20]{4,1,3,0,2:T(8,128)(2,1)S(1)} %bitcast.560, bf16[8,6,64,20]{2,3,1,0:T(8,128)(2,1)S(1)} %copy-done.4, ...), kind=kOutput, calls=%fused_computation.60.clone.1 | convolution fusion | flops 34077824 | bytes 749568 | tf_op jit(solution)/shard_map/while/body/eval_jaxpr/nhqk,nhkd->nhqd/dot_general | solution.py:62
  303.8 3.9 fusion.424
  324.4 5.7 %convolution_convert_fusion.14 = bf16[8,6,64,20]{2,3,1,0:T(8,128)(2,1)S(1)} fusion(f32[8,6,64]{2,1,0:T(8,128)S(1)} %fusion.425, bf16[8,6,64,20]{2,3,1,0:T(8,128)(2,1)S(1)} %copy-done.2, bf16[8,6,64,20]{2,3,1,0:T(8,128)(2,1)S(1)} %copy.284, bf16[8,6,8,8,20]{4,1,3,0,2:T(8,128)(2,1)S(1)} %bitcast.560, bf16[8,6,64,20]{2,3,1,0:T(8,128)(2,1)S(1)} %copy-done.4, ...), kind=kOutput, calls=%fused_computation.60.clone.1 | convolution fusion | flops 34077824 | bytes 749568 | tf_op jit(solution)/shard_map/while/body/eval_jaxpr/nhqk,nhkd->nhqd/dot_general | solution.py:62
  335.8 3.9 fusion.424
  356.4 5.7 %convolution_convert_fusion.14 = bf16[8,6,64,20]{2,3,1,0:T(8,128)(2,1)S(1)} fusion(f32[8,6,64]{2,1,0:T(8,128)S(1)} %fusion.425, bf16[8,6,64,20]{2,3,1,0:T(8,128)(2,1)S(1)} %copy-done.2, bf16[8,6,64,20]{2,3,1,0:T(8,128)(2,1)S(1)} %copy.284, bf16[8,6,8,8,20]{4,1,3,0,2:T(8,128)(2,1)S(1)} %bitcast.560, bf16[8,6,64,20]{2,3,1,0:T(8,128)(2,1)S(1)} %copy-done.4, ...), kind=kOutput, calls=%fused_computation.60.clone.1 | convolution fusion | flops 34077824 | bytes 749568 | tf_op jit(solution)/shard_map/while/body/eval_jaxpr/nhqk,nhkd->nhqd/dot_general | solution.py:62
  367.8 3.9 fusion.424
  388.4 5.7 %convolution_convert_fusion.14 = bf16[8,6,64,20]{2,3,1,0:T(8,128)(2,1)S(1)} fusion(f32[8,6,64]{2,1,0:T(8,128)S(1)} %fusion.425, bf16[8,6,64,20]{2,3,1,0:T(8,128)(2,1)S(1)} %copy-done.2, bf16[8,6,64,20]{2,3,1,0:T(8,128)(2,1)S(1)} %copy.284, bf16[8,6,8,8,20]{4,1,3,0,2:T(8,128)(2,1)S(1)} %bitcast.560, bf16[8,6,64,20]{2,3,1,0:T(8,128)(2,1)S(1)} %copy-done.4, ...), kind=kOutput, calls=%fused_computation.60.clone.1 | convolution fusion | flops 34077824 | bytes 749568 | tf_op jit(solution)/shard_map/while/body/eval_jaxpr/nhqk,nhkd->nhqd/dot_general | solution.py:62
  399.9 5.8 %fusion.154 = bf16[120,8,256]{2,0,1:T(8,128)(2,1)} fusion(f32[120,8,256]{2,0,1:T(8,128)S(1)} %get-tuple-element.144, f32[8,256,240]{1,2,0:T(8,128)S(1)} %fusion.225, f32[8,256]{1,0:T(8,128)S(1)} %add_rsqrt_fusion, f32[8,256]{1,0:T(8,128)S(1)} %broadcast_multiply_fusion, bf16[2,240,120]{2,1,0:T(8,128)(2,1)S(1)} %copy-done.12, ...), kind=kOutput, calls=%fused_computation.172 | convolution fusion | flops 269598720 | bytes 4562944 | tf_op jit(solution)/shard_map/ck,crw->krw/dot_general | solution.py:40
  406.0 15.9 %collective-permute-done.4 = bf16[120,8,256]{2,0,1:T(8,128)(2,1)S(1)} collective-permute-done((bf16[120,8,256]{2,0,1:T(8,128)(2,1)}, bf16[120,8,256]{2,0,1:T(8,128)(2,1)S(1)}, u32[]{:S(2)}, u32[]{:S(2)}) %collective-permute-start.4) | collective-permute-done | bytes 491552 | tf_op jit(solution)/shard_map/ppermute | solution.py:29
  422.3 5.6 %collective-permute-done.5 = bf16[120,4,256]{2,0,1:T(8,128)(2,1)S(1)} collective-permute-done((bf16[120,4,256]{2,0,1:T(8,128)(2,1)S(1)}, bf16[120,4,256]{2,0,1:T(8,128)(2,1)S(1)}, u32[]{:S(2)}, u32[]{:S(2)}) %collective-permute-start.5) | collective-permute-done | bytes 245792 | tf_op jit(solution)/shard_map/ppermute | solution.py:29
  (395 shorter events, 193.5 us)
Async XLA Ops:
  2.3 1.8 copy-start
  2.4 1.8 copy-start.6
  6.2 46.1 %collective-permute-start = (bf16[480,8,256]{2,0,1:T(8,128)(2,1)}, bf16[480,8,256]{2,0,1:T(8,128)(2,1)}, u32[]{:S(2)}, u32[]{:S(2)}) collective-permute-start(bf16[480,8,256]{2,0,1:T(8,128)(2,1)} %pad_maximum_fusion), channel_id=1, source_target_pairs={{0,4},{4,0},{8,12},{12,8},{16,20},{20,16},{24,28},{28,24},{1,5},{5... | collective-permute-start | bytes 5898248 | tf_op jit(solution)/shard_map/ppermute | solution.py:23
  78.3 2.6 copy-start.1
  78.3 2.7 copy-start.3
  110.3 2.6 copy-start.1
  110.3 2.6 copy-start.3
  142.3 2.6 copy-start.1
  142.3 2.6 copy-start.3
  174.3 2.6 copy-start.1
  174.3 2.7 copy-start.3
  185.9 1.4 copy-start.8
  187.2 0.9 copy-start.10
  194.5 20.3 %copy-start.5 = (bf16[2,120,360]{2,1,0:T(8,128)(2,1)S(1)}, bf16[2,120,360]{2,1,0:T(8,128)(2,1)}, u32[]{:S(2)}) copy-start(bf16[2,120,360]{2,1,0:T(8,128)(2,1)} %param.13) | copy-start | bytes 518404
  194.5 4.1 collective-permute-start.1
  199.1 15.5 %collective-permute-start.2 = (bf16[120,8,256]{2,0,1:T(8,128)(2,1)S(1)}, bf16[120,8,256]{2,0,1:T(8,128)(2,1)S(1)}, u32[]{:S(2)}, u32[]{:S(2)}) collective-permute-start(bf16[120,8,256]{2,0,1:T(8,128)(2,1)S(1)} %fusion.229), channel_id=1, source_target_pairs={{0,28},{4,0},{8,4},{12,8},{16,12},{20,16},{24,20},{28,24},{1,29},{... | collective-permute-start | bytes 1474568 | tf_op jit(solution)/shard_map/ppermute | solution.py:29
  214.8 0.9 copy-start.7
  217.8 45.9 %collective-permute-start.3 = (bf16[480,8,256]{2,0,1:T(8,128)(2,1)}, bf16[480,8,256]{2,0,1:T(8,128)(2,1)}, u32[]{:S(2)}, u32[]{:S(2)}) collective-permute-start(bf16[480,8,256]{2,0,1:T(8,128)(2,1)} %pad_maximum_fusion.1), channel_id=1, source_target_pairs={{0,4},{4,0},{8,12},{12,8},{16,20},{20,16},{24,28},{28,24},{1,5},{5... | collective-permute-start | bytes 5898248 | tf_op jit(solution)/shard_map/ppermute | solution.py:23
  289.7 2.6 copy-start.2
  289.7 2.7 copy-start.4
  321.7 2.6 copy-start.2
  321.7 2.7 copy-start.4
  353.7 2.6 copy-start.2
  353.7 2.6 copy-start.4
  385.7 2.6 copy-start.2
  385.7 2.7 copy-start.4
  397.1 1.4 copy-start.9
  398.4 0.9 copy-start.11
  399.0 0.9 copy-start.12
  399.0 1.0 copy-start.13
  405.7 16.2 %collective-permute-start.4 = (bf16[120,8,256]{2,0,1:T(8,128)(2,1)}, bf16[120,8,256]{2,0,1:T(8,128)(2,1)S(1)}, u32[]{:S(2)}, u32[]{:S(2)}) collective-permute-start(bf16[120,8,256]{2,0,1:T(8,128)(2,1)} %fusion.154), channel_id=1, source_target_pairs={{0,4},{4,8},{8,12},{12,16},{16,20},{20,24},{24,28},{28,0},{1,5},{5... | collective-permute-start | bytes 1474568 | tf_op jit(solution)/shard_map/ppermute | solution.py:29
  422.2 5.7 %collective-permute-start.5 = (bf16[120,4,256]{2,0,1:T(8,128)(2,1)S(1)}, bf16[120,4,256]{2,0,1:T(8,128)(2,1)S(1)}, u32[]{:S(2)}, u32[]{:S(2)}) collective-permute-start(bf16[120,4,256]{2,0,1:T(8,128)(2,1)S(1)} %fusion.248), channel_id=1, source_target_pairs={{0,1},{1,2},{2,3},{3,0},{4,5},{5,6},{6,7},{7,4},{8,9},{9,10},{10,1... | collective-permute-start | bytes 737288 | tf_op jit(solution)/shard_map/ppermute | solution.py:29
where the time goes:
time: 433 us; the launch traced here: 429 us
  local copies, waits for them, and re-layouts  161 us (37%)
  matrix products  119 us (27%)
  waiting for transfers between devices  119 us (27%)
  other arithmetic  13.1 us (3%)
  starting transfers between devices  8.61 us (2%)
  loops' own time  8.09 us (2%)
    ppermute x2, waiting for transfers between devices, swapped(): return lax.ppermute(block, axis, route)  82.4 us
    dot_general x16, matrix products, window_mix(): jnp.einsum('nhqk,nhkd->nhqd', weights, values, preferred_element_type=jnp...  65.4 us
    ppermute x4, waiting for transfers between devices, from_behind(): return lax.ppermute(value, axis, pairs)  36.2 us
    reshape x64, local copies, waits for them, and re-layouts, to_windows(): shaped = strip_data.reshape(HEADS, HEAD, WIN, win_count, WIN)  34 us
    slice x8, local copies, waits for them, and re-layouts, column_block(): other_kv[:C]  30.9 us
    reshape x32, local copies, waits for them, and re-layouts, to_windows(): shaped.transpose(3, 0, 2, 4, 1).reshape(win_count, HEADS, WIN * WIN, HEAD)  23.9 us
    sub x16, matrix products, window_mix(): weights = jnp.exp(scores - row_max)  22.8 us
    dot_general x10, matrix products, project(): jnp.einsum('ck,crw->krw', weight, values, preferred_element_type=jnp.floa...  17 us
  transfers between devices with their start and end apart: 6, of which 6 were waited for; matrix products, arithmetic and copies ran while one was open for 1% of the time, Pallas kernels for 0%

commit v1 on v0

v1 whole, which is shorter than its diff:
```python
import math

import jax
import jax.numpy as jnp
from jax import lax
from jax.experimental import pallas as pl
from jax.experimental.pallas import tpu as pltpu
from jax.sharding import PartitionSpec as P

C = 120
HEADS = 6
HEAD = 20
FFN = 240
WIN = 8
TOK = WIN * WIN
LANES = 128
PAIR = 2 * HEAD
GROUP = 48
VROWS = 3 * GROUP
CHUNK = 64
epsilon = 1e-05
f32 = jnp.float32
bf16 = jnp.bfloat16


def nn(a, b):
    return lax.dot_general(a, b, (((1,), (0,)), ((), ())), preferred_element_type=f32)


def nt(a, b):
    return lax.dot_general(a, b, (((1,), (1,)), ((), ())), preferred_element_type=f32)


def normed(values, axis):
    centred = values - jnp.mean(values, axis=axis, keepdims=True)
    spread = jnp.mean(centred * centred, axis=axis, keepdims=True)
    return (centred * lax.rsqrt(spread + epsilon)).astype(bf16)


def window_tokens(block):
    wins = block.shape[1] // WIN
    shaped = block.astype(f32).reshape(WIN, wins, WIN, C)
    return shaped.transpose(1, 0, 2, 3).reshape(wins * TOK, C)


def gelu(values):
    return 0.5 * values * (1.0 + lax.erf(values * (0.5 ** 0.5)))


def layer_chunk(x_tok, p_tok, wq, wk, wv, wpm, wps, wgu, wd):
    tokens = x_tok.shape[0]
    own = normed(x_tok, 1)
    other = normed(p_tok, 1)
    q_t = nt(wq, own)
    k_own = nn(own, wk[:, LANES:]).astype(bf16)
    k_other = nn(other, wk).astype(bf16)
    v_own = nt(wv[VROWS:], own)
    v_other = nt(wv, other)

    low = lax.broadcasted_iota(jnp.int32, (1, LANES), 1) < TOK
    row = lax.broadcasted_iota(jnp.int32, (LANES, LANES), 0)
    lane = lax.broadcasted_iota(jnp.int32, (LANES, LANES), 1)
    head_of = jnp.where(lane < TOK, 0, 1)
    masks = jnp.concatenate(
        [
            ((row >= PAIR * j + HEAD * head_of) & (row < PAIR * j + HEAD * head_of + HEAD))
            .astype(f32).astype(bf16)
            for j in range(3)
        ],
        axis=1,
    )
    first_head = lax.broadcasted_iota(jnp.int32, (C, LANES), 0) % PAIR < HEAD
    factor = HEAD ** (-0.5) * math.log2(math.e)

    def score(keys, query):
        return nn(keys, jnp.concatenate([query.astype(bf16)] * 3, axis=1) * masks)

    def soften(scores):
        top = jnp.max(scores, axis=0, keepdims=True)
        weights = jnp.exp2((scores - top) * factor)
        return (weights * (1.0 / jnp.sum(weights, axis=0, keepdims=True))).astype(bf16)

    def gather(values, weights):
        parts = [
            nn(values[GROUP * j : GROUP * (j + 1)], weights[:, LANES * j : LANES * (j + 1)])
            for j in range(3)
        ]
        return jnp.concatenate([part[:PAIR] for part in parts], axis=0)

    def swap(block):
        return pltpu.roll(block, TOK, 1)

    def merge(first, second):
        return jnp.where(
            first_head,
            jnp.where(low, first, swap(second)),
            jnp.where(low, swap(first), second),
        ).astype(bf16)

    def scores_of(pair):
        cols = slice(LANES * pair, LANES * (pair + 1))
        rows_a = slice(LANES * pair, LANES * pair + TOK)
        rows_b = slice(LANES * pair + TOK, LANES * (pair + 1))
        q_m, q_s = q_t[:LANES, cols], q_t[LANES:, cols]
        q_m_r, q_s_r = swap(q_m), swap(q_s)
        return [
            score(k_other[rows_a, :LANES], jnp.where(low, q_m, q_m_r)),
            score(k_other[rows_b, :LANES], jnp.where(low, q_m_r, q_m)),
            score(
                jnp.concatenate([k_own[rows_a], k_other[rows_a, LANES:]], axis=0),
                jnp.where(low, q_s, q_s_r),
            ),
            score(
                jnp.concatenate([k_own[rows_b], k_other[rows_b, LANES:]], axis=0),
                jnp.where(low, q_s_r, q_s),
            ),
        ]

    def mixed(pair, weights):
        cols = slice(LANES * pair, LANES * (pair + 1))
        vo, vp_m, vp_s = v_own[:, cols], v_other[:VROWS, cols], v_other[VROWS:, cols]
        vo_r, vp_m_r, vp_s_r = swap(vo), swap(vp_m), swap(vp_s)
        mut_a = gather(vp_m[:, :TOK].astype(bf16), weights[0])
        mut_b = gather(vp_m_r[:, :TOK].astype(bf16), weights[1])
        self_a = gather(jnp.where(low, vo, vp_s_r).astype(bf16), weights[2])
        self_b = gather(jnp.where(low, vo_r, vp_s).astype(bf16), weights[3])
        return merge(mut_a, mut_b), merge(self_a, self_b)

    pairs = tokens // LANES
    scores, weights, mutual, selfish = {}, {}, [], []
    for step in range(pairs + 2):
        if step < pairs:
            scores[step] = scores_of(step)
        if 0 <= step - 1 < pairs:
            weights[step - 1] = [soften(one) for one in scores.pop(step - 1)]
        if step >= 2:
            first, second = mixed(step - 2, weights.pop(step - 2))
            mutual.append(first)
            selfish.append(second)
    mutual = jnp.concatenate(mutual, axis=1)
    selfish = jnp.concatenate(selfish, axis=1)

    eye = (
        lax.broadcasted_iota(jnp.int32, (C, C), 0) == lax.broadcasted_iota(jnp.int32, (C, C), 1)
    ).astype(f32).astype(bf16)
    middle = nt(eye, x_tok.astype(bf16)) + (nn(wpm, mutual) + nn(wps, selfish))
    second = normed(middle, 0)
    gate_up = nn(wgu, second)
    hidden = (gelu(gate_up[:FFN]) * gate_up[FFN:]).astype(bf16)
    return middle + nn(wd, hidden)


def layer_result(x_tok, p_tok, layer, wq, wk, wv, wpm, wps, wgu, wd):
    result = layer_chunk(
        x_tok, p_tok, wq[layer], wk[layer], wv[layer], wpm[layer], wps[layer], wgu[layer],
        wd[layer],
    )
    wins = CHUNK // WIN
    back = result.T.reshape(wins, WIN, WIN, C).transpose(1, 0, 2, 3)
    return back.reshape(WIN, CHUNK, C).astype(bf16)


def arrange_weights(layer, w_mut, w_slf, w_prj, w_gte, w_upp, w_dwn, wq, wk, wv, wpm, wps, wgu, wd):
    blank = jnp.zeros((LANES - C, C), f32)
    for part, source in enumerate((w_mut, w_slf)):
        whole = source[layer].astype(f32)
        turned = whole.T
        wq[layer, LANES * part : LANES * (part + 1)] = jnp.concatenate(
            [turned[:C], blank], axis=0
        ).astype(bf16)
        wk[layer, :, LANES * part : LANES * part + C] = whole[:, C : 2 * C].astype(bf16)
        rows = []
        for j in range(3):
            rows += [turned[2 * C + PAIR * j : 2 * C + PAIR * (j + 1)], blank]
        wv[layer, VROWS * part : VROWS * (part + 1)] = jnp.concatenate(rows, axis=0).astype(bf16)
    joint = w_prj[layer].astype(f32)
    wpm[layer] = joint[:C].T.astype(bf16)
    wps[layer] = joint[C:].T.astype(bf16)
    wgu[layer, :FFN] = w_gte[layer].astype(f32).T.astype(bf16)
    wgu[layer, FFN:] = w_upp[layer].astype(f32).T.astype(bf16)
    wd[layer] = w_dwn[layer].astype(f32).T.astype(bf16)


def both_layers(
    x_ref, w_mut, w_slf, w_prj, w_gte, w_upp, w_dwn, out_ref,
    partner, upper, lower, from_below, mate_lower, mate_upper, result_low,
    wq, wk, wv, wpm, wps, wgu, wd, send, recv,
):
    half = WIN // 2
    cols = x_ref.shape[1]
    chunks = cols // CHUNK
    wide = CHUNK + 16
    frames, strips = lax.axis_size("frame"), lax.axis_size("strip")
    f, s = lax.axis_index("frame"), lax.axis_index("strip")
    odd = lax.rem(f, 2)
    twin = f + 1 - 2 * odd
    mate = lax.rem(f + 2 * odd - 1 + frames, frames)
    above = lax.rem(s + strips - 1, strips)
    below = lax.rem(s + 1, strips)

    def span(c, width=CHUNK):
        return pl.ds(pl.multiple_of(c * CHUNK, CHUNK), width)

    def copy(group, c):
        source, target, device = (
            (x_ref, partner, (twin, s)),
            (upper, from_below, (f, above)),
            (lower, mate_lower, (mate, s)),
            (upper, mate_upper, (mate, above)),
            (result_low, out_ref, (f, below)),
        )[group]
        rows = pl.ds(0, WIN if group == 0 else half)
        return pltpu.make_async_remote_copy(
            src_ref=source.at[rows, span(c), :],
            dst_ref=target.at[rows, span(c), :],
            send_sem=send.at[group, c],
            recv_sem=recv.at[group, c],
            device_id=device,
            device_id_type=pl.DeviceIdType.MESH,
        )

    barrier = pltpu.get_barrier_semaphore()
    known = [(twin, s), (mate, s), (f, above), (f, below), (mate, above), (mate, below)]
    for device in known:
        pl.semaphore_signal(
            barrier, inc=1, device_id=device, device_id_type=pl.DeviceIdType.MESH
        )
    pl.semaphore_wait(barrier, len(known))
    for c in range(chunks):
        copy(0, c).start()

    wk[...] = jnp.zeros_like(wk)
    raw = (w_mut, w_slf, w_prj, w_gte, w_upp, w_dwn)
    ready = (wq, wk, wv, wpm, wps, wgu, wd)
    for layer in range(2):
        arrange_weights(layer, *raw, *ready)

    @pl.loop(0, chunks)
    def _(c):
        copy(0, c).wait_recv()
        here = layer_result(
            window_tokens(x_ref[:, span(c), :]), window_tokens(partner[:, span(c), :]), 0, *ready
        )
        upper[:, span(c), :] = here[:half]
        lower[:, span(c), :] = here[half:]
        for group in (2, 3, 1):
            copy(group, c).start()

    for group in (2, 3, 1):
        copy(group, 0).wait_recv()
    for held in (lower, from_below, mate_lower, mate_upper):
        held[:, cols : cols + 16, :] = held[:, :16, :]

    def shifted(top, bottom, c):
        joined = jnp.concatenate([top[:, span(c, wide), :], bottom[:, span(c, wide), :]], axis=0)
        return window_tokens(joined.astype(f32)[:, half : half + CHUNK, :])

    @pl.loop(0, chunks)
    def _(c):
        @pl.when(c < chunks - 1)
        def _():
            for group in (2, 3, 1):
                copy(group, c + 1).wait_recv()

        here = layer_result(
            shifted(lower, from_below, c), shifted(mate_lower, mate_upper, c), 1, *ready
        )
        out_ref[half:, span(c), :] = here[:half]
        result_low[:, span(c), :] = here[half:]
        copy(4, c).start()

    for c in range(chunks):
        copy(4, c).wait_recv()
        for group in range(5):
            copy(group, c).wait_send()


def on_device(features, w_mutual, w_self, w_proj, w_gate, w_up, w_down):
    half = WIN // 2
    current = features[0].transpose(1, 2, 0)
    cols = current.shape[1]
    chunks = cols // CHUNK
    held = pltpu.VMEM((half, cols + 16, C), bf16)
    plain = pltpu.VMEM((half, cols, C), bf16)
    in_vmem = pl.BlockSpec(memory_space=pltpu.VMEM)
    result = pl.pallas_call(
        both_layers,
        in_specs=[in_vmem] * 7,
        out_specs=in_vmem,
        out_shape=jax.ShapeDtypeStruct(current.shape, bf16),
        scratch_shapes=[
            pltpu.VMEM((WIN, cols, C), bf16),
            plain,
            held,
            held,
            held,
            held,
            plain,
            pltpu.VMEM((2, 2 * LANES, C), bf16),
            pltpu.VMEM((2, C, 2 * LANES), bf16),
            pltpu.VMEM((2, 2 * VROWS, C), bf16),
            pltpu.VMEM((2, C, C), bf16),
            pltpu.VMEM((2, C, C), bf16),
            pltpu.VMEM((2, 2 * FFN, C), bf16),
            pltpu.VMEM((2, C, FFN), bf16),
            pltpu.SemaphoreType.DMA((5, chunks)),
            pltpu.SemaphoreType.DMA((5, chunks)),
        ],
        compiler_params=pltpu.CompilerParams(
            vmem_limit_bytes=48 * 1024 * 1024, collective_id=0, has_side_effects=True
        ),
        cost_estimate=pl.CostEstimate(
            flops=2_400_000_000, bytes_accessed=3_000_000, transcendentals=6_000_000
        ),
    )(current, w_mutual, w_self, w_proj, w_gate, w_up, w_down)
    return jnp.roll(result, half, axis=1).transpose(2, 0, 1)[None]


def solution(mesh):
    in_specs = (P("frame", None, "strip", None), P(), P(), P(), P(), P(), P())
    out_specs = P("frame", None, "strip", None)
    return jax.shard_map(
        on_device, mesh=mesh, in_specs=in_specs, out_specs=out_specs, check_vma=False
    )
```

time: 433 us -> 49 us (0.11)
  local copies, waits for them, and re-layouts: 161 us -> 2.71 us
  matrix products: 119 us -> 0 us
  waiting for transfers between devices: 119 us -> 0 us
  Pallas kernels: 0 us -> 45 us
  other arithmetic: 13.1 us -> 0.18 us
  starting transfers between devices: 8.61 us -> 0 us
  loops' own time: 8.09 us -> 0 us
    ppermute x6 -> x0, waiting for transfers between devices: 119 us -> none  [the longest x2 82.4 us: swapped(): return lax.ppermute(block, axis, route)]
    dot_general x34 -> x0, matrix products: 96 us -> none  [the longest x16 65.4 us: window_mix(): jnp.einsum('nhqk,nhkd->nhqd', weights, values, preferred_element_type=jnp...]
    reshape x112 -> x0, local copies, waits for them, and re-layouts: 67 us -> none  [the longest x64 34 us: to_windows(): shaped = strip_data.reshape(HEADS, HEAD, WIN, win_count, WIN)]
    pallas_call x0 -> x1, Pallas kernels: none -> 45 us  [on_device(): pl.pallas_call(both_layers, in_specs=[in_vmem] * 7, out_specs=in_vmem, ou...]
    slice x22 -> x1, local copies, waits for them, and re-layouts: 39.9 us -> 0.01 us  [on_device(): return jnp.roll(result, half, axis=1).transpose(2, 0, 1)[None]]
    transpose x50 -> x0, local copies, waits for them, and re-layouts: 24.1 us -> none  [the longest x16 15.2 us: from_windows(): shaped.transpose(1, 4, 2, 0, 3).reshape(HEADS * HEAD, WIN, win_count * WIN)]
    sub x16 -> x0, matrix products: 22.8 us -> none  [window_mix(): weights = jnp.exp(scores - row_max)]
    while x38 -> x0, local copies, waits for them, and re-layouts: 14.1 us -> none  [the longest x6 14 us: attend(): blocks = lax.map(column_block, jnp.arange(block_count, dtype=jnp.int32))]
  transfers between devices with their start and end apart: 6 -> 0, of which waited for: 6 -> 0; matrix products, arithmetic and copies ran while one was open for 1% -> 0% of each run, Pallas kernels for 0% -> 0%
where the time goes in v1:
time: 49 us; the launch traced here: 48 us
  Pallas kernels  45 us (92%)
  local copies, waits for them, and re-layouts  2.71 us (6%)
    pallas_call x1, Pallas kernels, on_device(): pl.pallas_call(both_layers, in_specs=[in_vmem] * 7, out_specs=in_vmem, ou...  45 us
    unnamed x13, local copies, waits for them, and re-layouts  1.54 us
    broadcast_in_dim x1, local copies, waits for them, and re-layouts, on_device(): return jnp.roll(result, half, axis=1).transpose(2, 0, 1)[None]  1.17 us

profile of v1, /device:TPU:0, one launch (start us, length us, event | category | flops | bytes accessed | tf_op | source)
XLA Modules:
  0.0 48.0 jit_solution(13957512199427422972)
XLA Ops:
  0.0 0.0 copy-start.5
  0.0 0.0 copy-start.4
  0.0 0.0 copy-start.3
  0.0 0.0 copy-start.2
  0.0 0.0 copy-start.1
  0.0 0.0 copy-start
  0.0 1.5 %copy.8 = bf16[1,120,8,256]{1,3,2,0:T(8,128)(2,1)S(1)} copy(bf16[1,120,8,256]{3,2,1,0:T(8,128)(2,1)} %param.7) | data formatting | bytes 983040 | tf_op args[0]
  1.5 0.0 copy-done.5
  1.5 0.0 copy-done.4
  1.6 0.0 copy-done.3
  1.6 0.0 copy-done.2
  1.6 0.0 copy-done.1
  1.6 0.0 copy-done
  1.6 45.0 %shard_map.73 = bf16[8,256,120]{2,1,0:T(8,128)(2,1)S(1)} custom-call(bf16[8,256,120]{2,1,0:T(8,128)(2,1)S(1)} %bitcast.9, bf16[2,120,360]{2,1,0:T(8,128)(2,1)S(1)} %copy-done, bf16[2,120,360]{2,1,0:T(8,128)(2,1)S(1)} %copy-done.1, bf16[2,240,120]{2,1,0:T(8,128)(2,1)S(1)} %copy-done.2, bf16[2,120,240]{2,1,0:T(8,128)(2,1)S(1)} %copy-done.3, ...), custom_call_target="tpu_custom_call" | custom-call | flops 2400000000 | bytes 3000000 | tf_op jit(solution)/shard_map/pallas_call | solution.py:286
  46.6 0.2 maximum_bitcast_fusion
  46.8 1.2 %copy.9 = bf16[1,120,8,256]{3,2,1,0:T(8,128)(2,1)} copy(bf16[1,120,8,256]{1,3,2,0:T(8,128)(2,1)S(1)} %maximum_bitcast_fusion) | data formatting | bytes 983040 | tf_op jit(solution)/shard_map/broadcast_in_dim | solution.py:316
  (1 shorter events, 0.0 us)
Async XLA Ops:
  0.0 1.5 %copy-start.5 = (bf16[2,240,120]{2,1,0:T(8,128)(2,1)S(1)}, bf16[2,240,120]{2,1,0:T(8,128)(2,1)}, u32[]{:S(2)}) copy-start(bf16[2,240,120]{2,1,0:T(8,128)(2,1)} %w_dwn.1) | copy-start | bytes 345604
  0.0 1.5 %copy-start.4 = (bf16[2,120,240]{2,1,0:T(8,128)(2,1)S(1)}, bf16[2,120,240]{2,1,0:T(8,128)(2,1)}, u32[]{:S(2)}) copy-start(bf16[2,120,240]{2,1,0:T(8,128)(2,1)} %w_upp.1) | copy-start | bytes 345604
  0.0 1.6 %copy-start.3 = (bf16[2,120,240]{2,1,0:T(8,128)(2,1)S(1)}, bf16[2,120,240]{2,1,0:T(8,128)(2,1)}, u32[]{:S(2)}) copy-start(bf16[2,120,240]{2,1,0:T(8,128)(2,1)} %w_gte.1) | copy-start | bytes 345604
  0.0 1.6 %copy-start.2 = (bf16[2,240,120]{2,1,0:T(8,128)(2,1)S(1)}, bf16[2,240,120]{2,1,0:T(8,128)(2,1)}, u32[]{:S(2)}) copy-start(bf16[2,240,120]{2,1,0:T(8,128)(2,1)} %w_prj.1) | copy-start | bytes 345604
  0.0 1.6 %copy-start.1 = (bf16[2,120,360]{2,1,0:T(8,128)(2,1)S(1)}, bf16[2,120,360]{2,1,0:T(8,128)(2,1)}, u32[]{:S(2)}) copy-start(bf16[2,120,360]{2,1,0:T(8,128)(2,1)} %w_slf.1) | copy-start | bytes 518404
  0.0 1.6 %copy-start = (bf16[2,120,360]{2,1,0:T(8,128)(2,1)S(1)}, bf16[2,120,360]{2,1,0:T(8,128)(2,1)}, u32[]{:S(2)}) copy-start(bf16[2,120,360]{2,1,0:T(8,128)(2,1)} %w_mut.1) | copy-start | bytes 518404

commit v2 on v1

v2 whole, which is shorter than its diff:
```python
import math

import jax
import jax.numpy as jnp
from jax import lax
from jax.experimental import pallas as pl
from jax.experimental.pallas import tpu as pltpu
from jax.sharding import PartitionSpec as P

C = 120
HEADS = 6
HEAD = 20
FFN = 240
WIN = 8
TOK = WIN * WIN
LANES = 128
PAIR = 2 * HEAD
GROUP = 48
VROWS = 3 * GROUP
CHUNK = 32
SLACK = 16
epsilon = 1e-05
f32 = jnp.float32
bf16 = jnp.bfloat16


def nn(a, b):
    return lax.dot_general(a, b, (((1,), (0,)), ((), ())), preferred_element_type=f32)


def nt(a, b):
    return lax.dot_general(a, b, (((1,), (1,)), ((), ())), preferred_element_type=f32)


def normed(values, axis):
    centred = values - jnp.mean(values, axis=axis, keepdims=True)
    spread = jnp.mean(centred * centred, axis=axis, keepdims=True)
    return (centred * lax.rsqrt(spread + epsilon)).astype(bf16)


def window_tokens(block):
    wins = block.shape[1] // WIN
    shaped = block.astype(f32).reshape(WIN, wins, WIN, C)
    return shaped.transpose(1, 0, 2, 3).reshape(wins * TOK, C)


def gelu(values):
    return 0.5 * values * (1.0 + lax.erf(values * (0.5 ** 0.5)))


def layer_chunk(x_tok, wq, wk, wv, wpm, wps, wgu, wd):
    tokens = x_tok.shape[0]
    normal = normed(x_tok, 1)
    q_t = nt(wq, normal)
    keys = nn(normal, wk).astype(bf16)
    values = nt(wv, normal)
    pairs = tokens // LANES

    low = lax.broadcasted_iota(jnp.int32, (1, LANES), 1) < TOK
    row = lax.broadcasted_iota(jnp.int32, (LANES, LANES), 0)
    lane = lax.broadcasted_iota(jnp.int32, (LANES, LANES), 1)
    head_of = jnp.where(lane < TOK, 0, 1)
    masks = jnp.concatenate(
        [
            ((row >= PAIR * j + HEAD * head_of) & (row < PAIR * j + HEAD * head_of + HEAD))
            .astype(f32).astype(bf16)
            for j in range(3)
        ],
        axis=1,
    )
    first_head = lax.broadcasted_iota(jnp.int32, (C, LANES), 0) % PAIR < HEAD
    factor = HEAD ** (-0.5) * math.log2(math.e)

    def score(key_rows, query):
        return nn(key_rows, jnp.concatenate([query.astype(bf16)] * 3, axis=1) * masks)

    def soften(scores):
        top = jnp.max(scores, axis=0, keepdims=True)
        weights = jnp.exp2((scores - top) * factor)
        return (weights * (1.0 / jnp.sum(weights, axis=0, keepdims=True))).astype(bf16)

    def gather(value_rows, weights):
        parts = [
            nn(value_rows[GROUP * j : GROUP * (j + 1)], weights[:, LANES * j : LANES * (j + 1)])
            for j in range(3)
        ]
        return jnp.concatenate([part[:PAIR] for part in parts], axis=0)

    def swap(block):
        return pltpu.roll(block, TOK, 1)

    def merge(first, second):
        return jnp.where(
            first_head,
            jnp.where(low, first, swap(second)),
            jnp.where(low, swap(first), second),
        ).astype(bf16)

    def scores_of(pair):
        mate = (pair + pairs // 2) % pairs
        cols = slice(LANES * pair, LANES * (pair + 1))
        own_a = slice(LANES * pair, LANES * pair + TOK)
        own_b = slice(LANES * pair + TOK, LANES * (pair + 1))
        mate_a = slice(LANES * mate, LANES * mate + TOK)
        mate_b = slice(LANES * mate + TOK, LANES * (mate + 1))
        q_m, q_s = q_t[:LANES, cols], q_t[LANES:, cols]
        q_m_r, q_s_r = swap(q_m), swap(q_s)
        return [
            score(keys[mate_a, :LANES], jnp.where(low, q_m, q_m_r)),
            score(keys[mate_b, :LANES], jnp.where(low, q_m_r, q_m)),
            score(
                jnp.concatenate([keys[own_a, LANES:], keys[mate_a, LANES:]], axis=0),
                jnp.where(low, q_s, q_s_r),
            ),
            score(
                jnp.concatenate([keys[own_b, LANES:], keys[mate_b, LANES:]], axis=0),
                jnp.where(low, q_s_r, q_s),
            ),
        ]

    def mixed(pair, weights):
        mate = (pair + pairs // 2) % pairs
        cols = slice(LANES * pair, LANES * (pair + 1))
        mate_cols = slice(LANES * mate, LANES * (mate + 1))
        v_own, v_m, v_s = values[VROWS:, cols], values[:VROWS, mate_cols], values[VROWS:, mate_cols]
        mut_a = gather(v_m[:, :TOK].astype(bf16), weights[0])
        mut_b = gather(swap(v_m)[:, :TOK].astype(bf16), weights[1])
        self_a = gather(jnp.where(low, v_own, swap(v_s)).astype(bf16), weights[2])
        self_b = gather(jnp.where(low, swap(v_own), v_s).astype(bf16), weights[3])
        return merge(mut_a, mut_b), merge(self_a, self_b)

    scores, weights, mutual, selfish = {}, {}, [], []
    for step in range(pairs + 2):
        if step < pairs:
            scores[step] = scores_of(step)
        if 0 <= step - 1 < pairs:
            weights[step - 1] = [soften(one) for one in scores.pop(step - 1)]
        if step >= 2:
            first, second = mixed(step - 2, weights.pop(step - 2))
            mutual.append(first)
            selfish.append(second)
    mutual = jnp.concatenate(mutual, axis=1)
    selfish = jnp.concatenate(selfish, axis=1)

    eye = (
        lax.broadcasted_iota(jnp.int32, (C, C), 0) == lax.broadcasted_iota(jnp.int32, (C, C), 1)
    ).astype(f32).astype(bf16)
    middle = nt(eye, x_tok.astype(bf16)) + (nn(wpm, mutual) + nn(wps, selfish))
    second = normed(middle, 0)
    gate_up = nn(wgu, second)
    hidden = (gelu(gate_up[:FFN]) * gate_up[FFN:]).astype(bf16)
    return middle + nn(wd, hidden)


def layer_result(first, second, layer, wq, wk, wv, wpm, wps, wgu, wd):
    tokens = jnp.concatenate([window_tokens(first), window_tokens(second)], axis=0)
    result = layer_chunk(
        tokens, wq[layer], wk[layer], wv[layer], wpm[layer], wps[layer], wgu[layer], wd[layer]
    )
    wins = CHUNK // WIN
    back = result.T.reshape(2, wins, WIN, WIN, C).transpose(0, 2, 1, 3, 4)
    back = back.reshape(2, WIN, CHUNK, C).astype(bf16)
    return back[0], back[1]


def arrange_weights(layer, w_mut, w_slf, w_prj, w_gte, w_upp, w_dwn, wq, wk, wv, wpm, wps, wgu, wd):
    blank = jnp.zeros((LANES - C, C), f32)
    for part, source in enumerate((w_mut, w_slf)):
        whole = source[layer].astype(f32)
        turned = whole.T
        wq[layer, LANES * part : LANES * (part + 1)] = jnp.concatenate(
            [turned[:C], blank], axis=0
        ).astype(bf16)
        wk[layer, :, LANES * part : LANES * part + C] = whole[:, C : 2 * C].astype(bf16)
        rows = []
        for j in range(3):
            rows += [turned[2 * C + PAIR * j : 2 * C + PAIR * (j + 1)], blank]
        wv[layer, VROWS * part : VROWS * (part + 1)] = jnp.concatenate(rows, axis=0).astype(bf16)
    joint = w_prj[layer].astype(f32)
    wpm[layer] = joint[:C].T.astype(bf16)
    wps[layer] = joint[C:].T.astype(bf16)
    wgu[layer, :FFN] = w_gte[layer].astype(f32).T.astype(bf16)
    wgu[layer, FFN:] = w_upp[layer].astype(f32).T.astype(bf16)
    wd[layer] = w_dwn[layer].astype(f32).T.astype(bf16)


def both_layers(
    x_ref, w_mut, w_slf, w_prj, w_gte, w_upp, w_dwn, out_ref,
    partner, upper, lower, halves, result,
    wq, wk, wv, wpm, wps, wgu, wd,
    send, recv, edge_send, edge_recv, out_send, out_recv,
):
    half = WIN // 2
    cols = x_ref.shape[1] // 2
    chunks = cols // CHUNK
    wide = CHUNK + SLACK
    couples, strips = lax.axis_size("frame") // 2, lax.axis_size("strip")
    f, s = lax.axis_index("frame"), lax.axis_index("strip")
    side = lax.rem(f, 2)
    couple = lax.div(f, 2)

    def at(d_couple, to_side, d_strip):
        to_couple = lax.rem(couple + d_couple + couples, couples)
        return (2 * to_couple + to_side, lax.rem(s + d_strip + strips, strips))

    def span(c, width=CHUNK):
        return pl.ds(pl.multiple_of(c * CHUNK, CHUNK), width)

    def place(c, which):
        return pl.ds(pl.multiple_of(which * cols + c * CHUNK, CHUNK), CHUNK)

    def remote(source, target, send_sem, recv_sem, device):
        return pltpu.make_async_remote_copy(
            src_ref=source,
            dst_ref=target,
            send_sem=send_sem,
            recv_sem=recv_sem,
            device_id=device,
            device_id_type=pl.DeviceIdType.MESH,
        )

    def copy(group, c):
        source, target, device = (
            (x_ref.at[:, place(c, 1 - side), :], partner.at[:, span(c), :], at(0, 1 - side, 0)),
            (upper.at[1, :, span(c), :], halves.at[1, :, span(c), :], at(0, side, -1)),
            (lower.at[0, :, span(c), :], halves.at[2, :, span(c), :], at(-1, side, 0)),
            (upper.at[0, :, span(c), :], halves.at[3, :, span(c), :], at(-1, side, -1)),
        )[group]
        return remote(source, target, send.at[group, c], recv.at[group, c], device)

    def edge(group):
        source, device = (
            (lower.at[1], at(0, 1 - side, 0)),
            (upper.at[1], at(0, 1 - side, -1)),
            (lower.at[0], at(-1, 1 - side, 0)),
            (upper.at[0], at(-1, 1 - side, -1)),
        )[group]
        return remote(
            source.at[:, pl.ds(0, SLACK), :],
            halves.at[group, :, pl.ds(cols, SLACK), :],
            edge_send.at[group],
            edge_recv.at[group],
            device,
        )

    def give_back(kind, c, origin):
        frame, part = kind // 2, kind % 2
        device = at(1 - frame, frame, part)
        return remote(
            result.at[1 - frame, pl.ds(half * part, half), span(c), :],
            out_ref.at[pl.ds(half * (1 - part), half), place(c, origin), :],
            out_send.at[kind, c],
            out_recv.at[part, origin, c],
            device,
        )

    barrier = pltpu.get_barrier_semaphore()
    known = [
        at(i, to_side, j)
        for i in (-1, 0, 1)
        for j in (-1, 0, 1)
        for to_side in ((1 - side,) if (i, j) == (0, 0) else (side, 1 - side))
    ]
    for device in known:
        pl.semaphore_signal(
            barrier, inc=1, device_id=device, device_id_type=pl.DeviceIdType.MESH
        )
    pl.semaphore_wait(barrier, len(known))

    copy(0, 0).start()
    wk[...] = jnp.zeros_like(wk)
    raw = (w_mut, w_slf, w_prj, w_gte, w_upp, w_dwn)
    ready = (wq, wk, wv, wpm, wps, wgu, wd)
    arrange_weights(0, *raw, *ready)
    for c in range(1, chunks):
        copy(0, c).start()
    arrange_weights(1, *raw, *ready)

    @pl.loop(0, chunks)
    def _(c):
        copy(0, c).wait_recv()
        own, other = layer_result(
            x_ref[:, place(c, side), :], partner[:, span(c), :], 0, *ready
        )
        upper[side, :, span(c), :] = own[:half]
        lower[side, :, span(c), :] = own[half:]
        upper[1 - side, :, span(c), :] = other[:half]
        lower[1 - side, :, span(c), :] = other[half:]
        for group in (2, 3, 1):
            copy(group, c).start()
        halves[0, :, span(c), :] = lower[1, :, span(c), :]

        @pl.when(c == 0)
        def _():
            for group in range(4):
                edge(group).start()

    for group in (2, 3, 1):
        copy(group, 0).wait_recv()

    def shifted(top, bottom, c):
        joined = jnp.concatenate(
            [halves[top, :, span(c, wide), :], halves[bottom, :, span(c, wide), :]], axis=0
        )
        return joined.astype(f32)[:, half : half + CHUNK, :]

    @pl.loop(0, chunks)
    def _(c):
        @pl.when(c < chunks - 1)
        def _():
            for group in (2, 3, 1):
                copy(group, c + 1).wait_recv()

        @pl.when(c == chunks - 1)
        def _():
            for group in range(4):
                edge(group).wait_recv()

        odd, even = layer_result(shifted(0, 1, c), shifted(2, 3, c), 1, *ready)
        result[0, :, span(c), :] = odd
        result[1, :, span(c), :] = even
        give_back(0, c, side).start()
        give_back(1, c, side).start()
        give_back(3, c, side).start()

        @pl.when(side == 0)
        def _():
            give_back(2, c, side).start()

        @pl.when(side == 1)
        def _():
            out_ref[half:, place(c, 1), :] = odd[:half]

    for c in range(chunks):
        give_back(0, c, 0).wait_recv()
        give_back(1, c, 0).wait_recv()
        give_back(1, c, 1).wait_recv()
        for kind in (0, 1, 3):
            give_back(kind, c, side).wait_send()
        for group in range(4):
            copy(group, c).wait_send()

    @pl.when(side == 0)
    def _():
        for c in range(chunks):
            give_back(0, c, 1).wait_recv()
            give_back(2, c, 0).wait_send()

    for group in range(4):
        edge(group).wait_send()


def on_device(features, w_mutual, w_self, w_proj, w_gate, w_up, w_down):
    half = WIN // 2
    current = features[0].transpose(1, 2, 0)
    cols = current.shape[1] // 2
    chunks = cols // CHUNK
    in_vmem = pl.BlockSpec(memory_space=pltpu.VMEM)
    result = pl.pallas_call(
        both_layers,
        in_specs=[in_vmem] * 7,
        out_specs=in_vmem,
        out_shape=jax.ShapeDtypeStruct(current.shape, bf16),
        scratch_shapes=[
            pltpu.VMEM((WIN, cols, C), bf16),
            pltpu.VMEM((2, half, cols, C), bf16),
            pltpu.VMEM((2, half, cols, C), bf16),
            pltpu.VMEM((4, half, cols + SLACK, C), bf16),
            pltpu.VMEM((2, WIN, cols, C), bf16),
            pltpu.VMEM((2, 2 * LANES, C), bf16),
            pltpu.VMEM((2, C, 2 * LANES), bf16),
            pltpu.VMEM((2, 2 * VROWS, C), bf16),
            pltpu.VMEM((2, C, C), bf16),
            pltpu.VMEM((2, C, C), bf16),
            pltpu.VMEM((2, 2 * FFN, C), bf16),
            pltpu.VMEM((2, C, FFN), bf16),
            pltpu.SemaphoreType.DMA((4, chunks)),
            pltpu.SemaphoreType.DMA((4, chunks)),
            pltpu.SemaphoreType.DMA((4,)),
            pltpu.SemaphoreType.DMA((4,)),
            pltpu.SemaphoreType.DMA((4, chunks)),
            pltpu.SemaphoreType.DMA((2, 2, chunks)),
        ],
        compiler_params=pltpu.CompilerParams(
            vmem_limit_bytes=48 * 1024 * 1024, collective_id=0, has_side_effects=True
        ),
        cost_estimate=pl.CostEstimate(
            flops=2_400_000_000, bytes_accessed=3_000_000, transcendentals=6_000_000
        ),
    )(current, w_mutual, w_self, w_proj, w_gate, w_up, w_down)
    return jnp.roll(result, half, axis=1).transpose(2, 0, 1)[None]


def solution(mesh):
    in_specs = (P("frame", None, "strip", None), P(), P(), P(), P(), P(), P())
    out_specs = P("frame", None, "strip", None)
    return jax.shard_map(
        on_device, mesh=mesh, in_specs=in_specs, out_specs=out_specs, check_vma=False
    )
```

time: 49 us -> 39.3 us (0.80); the launches traced: 48 us -> 39.2 us
  Pallas kernels: 45 us -> 36.2 us
    pallas_call x1, Pallas kernels: 45 us -> 36.2 us  [on_device(): pl.pallas_call(both_layers, in_specs=[in_vmem] * 7, out_specs=in_vmem, ou...]
where the time goes in v2:
time: 39.3 us; the launch traced here: 39.2 us
  Pallas kernels  36.2 us (92%)
  local copies, waits for them, and re-layouts  2.71 us (7%)
    pallas_call x1, Pallas kernels, on_device(): pl.pallas_call(both_layers, in_specs=[in_vmem] * 7, out_specs=in_vmem, ou...  36.2 us
    unnamed x13, local copies, waits for them, and re-layouts  1.54 us
    broadcast_in_dim x1, local copies, waits for them, and re-layouts, on_device(): return jnp.roll(result, half, axis=1).transpose(2, 0, 1)[None]  1.17 us

profile of v2, /device:TPU:0, one launch (start us, length us, event | category | flops | bytes accessed | tf_op | source)
XLA Modules:
  0.0 39.2 jit_solution(14719206154419013780)
XLA Ops:
  0.0 0.0 copy-start.5
  0.0 0.0 copy-start.4
  0.0 0.0 copy-start.3
  0.0 0.0 copy-start.2
  0.0 0.0 copy-start.1
  0.0 0.0 copy-start
  0.0 1.5 %copy.8 = bf16[1,120,8,256]{1,3,2,0:T(8,128)(2,1)S(1)} copy(bf16[1,120,8,256]{3,2,1,0:T(8,128)(2,1)} %param.7) | data formatting | bytes 983040 | tf_op args[0]
  1.5 0.0 copy-done.5
  1.5 0.0 copy-done.4
  1.6 0.0 copy-done.3
  1.6 0.0 copy-done.2
  1.6 0.0 copy-done.1
  1.6 0.0 copy-done
  1.6 36.2 %shard_map.73 = bf16[8,256,120]{2,1,0:T(8,128)(2,1)S(1)} custom-call(bf16[8,256,120]{2,1,0:T(8,128)(2,1)S(1)} %bitcast.9, bf16[2,120,360]{2,1,0:T(8,128)(2,1)S(1)} %copy-done, bf16[2,120,360]{2,1,0:T(8,128)(2,1)S(1)} %copy-done.1, bf16[2,240,120]{2,1,0:T(8,128)(2,1)S(1)} %copy-done.2, bf16[2,120,240]{2,1,0:T(8,128)(2,1)S(1)} %copy-done.3, ...), custom_call_target="tpu_custom_call" | custom-call | flops 2400000000 | bytes 3000000 | tf_op jit(solution)/shard_map/pallas_call | solution.py:359
  37.8 0.2 maximum_bitcast_fusion
  38.0 1.2 %copy.9 = bf16[1,120,8,256]{3,2,1,0:T(8,128)(2,1)} copy(bf16[1,120,8,256]{1,3,2,0:T(8,128)(2,1)S(1)} %maximum_bitcast_fusion) | data formatting | bytes 983040 | tf_op jit(solution)/shard_map/broadcast_in_dim | solution.py:391
  (1 shorter events, 0.0 us)
Async XLA Ops:
  0.0 1.5 %copy-start.5 = (bf16[2,240,120]{2,1,0:T(8,128)(2,1)S(1)}, bf16[2,240,120]{2,1,0:T(8,128)(2,1)}, u32[]{:S(2)}) copy-start(bf16[2,240,120]{2,1,0:T(8,128)(2,1)} %w_dwn.1) | copy-start | bytes 345604
  0.0 1.5 %copy-start.4 = (bf16[2,120,240]{2,1,0:T(8,128)(2,1)S(1)}, bf16[2,120,240]{2,1,0:T(8,128)(2,1)}, u32[]{:S(2)}) copy-start(bf16[2,120,240]{2,1,0:T(8,128)(2,1)} %w_upp.1) | copy-start | bytes 345604
  0.0 1.6 %copy-start.3 = (bf16[2,120,240]{2,1,0:T(8,128)(2,1)S(1)}, bf16[2,120,240]{2,1,0:T(8,128)(2,1)}, u32[]{:S(2)}) copy-start(bf16[2,120,240]{2,1,0:T(8,128)(2,1)} %w_gte.1) | copy-start | bytes 345604
  0.0 1.6 %copy-start.2 = (bf16[2,240,120]{2,1,0:T(8,128)(2,1)S(1)}, bf16[2,240,120]{2,1,0:T(8,128)(2,1)}, u32[]{:S(2)}) copy-start(bf16[2,240,120]{2,1,0:T(8,128)(2,1)} %w_prj.1) | copy-start | bytes 345604
  0.0 1.6 %copy-start.1 = (bf16[2,120,360]{2,1,0:T(8,128)(2,1)S(1)}, bf16[2,120,360]{2,1,0:T(8,128)(2,1)}, u32[]{:S(2)}) copy-start(bf16[2,120,360]{2,1,0:T(8,128)(2,1)} %w_slf.1) | copy-start | bytes 518404
  0.0 1.6 %copy-start = (bf16[2,120,360]{2,1,0:T(8,128)(2,1)S(1)}, bf16[2,120,360]{2,1,0:T(8,128)(2,1)}, u32[]{:S(2)}) copy-start(bf16[2,120,360]{2,1,0:T(8,128)(2,1)} %w_mut.1) | copy-start | bytes 518404

commit v3 on v2

--- a/solution.py
+++ b/solution.py
@@ -71,20 +71,47 @@
     first_head = lax.broadcasted_iota(jnp.int32, (C, LANES), 0) % PAIR < HEAD
     factor = HEAD ** (-0.5) * math.log2(math.e)
 
-    def score(key_rows, query):
-        return nn(key_rows, jnp.concatenate([query.astype(bf16)] * 3, axis=1) * masks)
+    def block_diagonal(first, second):
+        right = jnp.zeros((first.shape[0], second.shape[1]), bf16)
+        left = jnp.zeros((second.shape[0], first.shape[1]), bf16)
+        return jnp.concatenate(
+            [
+                jnp.concatenate([first, right], axis=1),
+                jnp.concatenate([left, second], axis=1),
+            ],
+            axis=0,
+        )
+
+    def spread(query):
+        return jnp.concatenate([query.astype(bf16)] * 3, axis=1) * masks
+
+    def score(own, mate, q_self, q_mut):
+        self_keys = jnp.concatenate([keys[own, LANES:], keys[mate, LANES:]], axis=0)
+        return nn(
+            block_diagonal(self_keys, keys[mate, :LANES]),
+            jnp.concatenate([spread(q_self), spread(q_mut)], axis=0),
+        )
 
     def soften(scores):
         top = jnp.max(scores, axis=0, keepdims=True)
         weights = jnp.exp2((scores - top) * factor)
         return (weights * (1.0 / jnp.sum(weights, axis=0, keepdims=True))).astype(bf16)
 
-    def gather(value_rows, weights):
+    def soften_both(scores):
+        return jnp.concatenate([soften(scores[: 2 * TOK]), soften(scores[2 * TOK :])], axis=0)
+
+    def gather(v_self, v_mut, weights):
         parts = [
-            nn(value_rows[GROUP * j : GROUP * (j + 1)], weights[:, LANES * j : LANES * (j + 1)])
+            nn(
+                block_diagonal(
+                    v_self[GROUP * j : GROUP * (j + 1)], v_mut[GROUP * j : GROUP * (j + 1)]
+                ),
+                weights[:, LANES * j : LANES * (j + 1)],
+            )
             for j in range(3)
         ]
-        return jnp.concatenate([part[:PAIR] for part in parts], axis=0)
+        selfish = jnp.concatenate([part[:PAIR] for part in parts], axis=0)
+        return selfish, jnp.concatenate([part[GROUP : GROUP + PAIR] for part in parts], axis=0)
 
     def swap(block):
         return pltpu.roll(block, TOK, 1)
@@ -106,16 +133,8 @@
         q_m, q_s = q_t[:LANES, cols], q_t[LANES:, cols]
         q_m_r, q_s_r = swap(q_m), swap(q_s)
         return [
-            score(keys[mate_a, :LANES], jnp.where(low, q_m, q_m_r)),
-            score(keys[mate_b, :LANES], jnp.where(low, q_m_r, q_m)),
-            score(
-                jnp.concatenate([keys[own_a, LANES:], keys[mate_a, LANES:]], axis=0),
-                jnp.where(low, q_s, q_s_r),
-            ),
-            score(
-                jnp.concatenate([keys[own_b, LANES:], keys[mate_b, LANES:]], axis=0),
-                jnp.where(low, q_s_r, q_s),
-            ),
+            score(own_a, mate_a, jnp.where(low, q_s, q_s_r), jnp.where(low, q_m, q_m_r)),
+            score(own_b, mate_b, jnp.where(low, q_s_r, q_s), jnp.where(low, q_m_r, q_m)),
         ]
 
     def mixed(pair, weights):
@@ -123,10 +142,14 @@
         cols = slice(LANES * pair, LANES * (pair + 1))
         mate_cols = slice(LANES * mate, LANES * (mate + 1))
         v_own, v_m, v_s = values[VROWS:, cols], values[:VROWS, mate_cols], values[VROWS:, mate_cols]
-        mut_a = gather(v_m[:, :TOK].astype(bf16), weights[0])
-        mut_b = gather(swap(v_m)[:, :TOK].astype(bf16), weights[1])
-        self_a = gather(jnp.where(low, v_own, swap(v_s)).astype(bf16), weights[2])
-        self_b = gather(jnp.where(low, swap(v_own), v_s).astype(bf16), weights[3])
+        self_a, mut_a = gather(
+            jnp.where(low, v_own, swap(v_s)).astype(bf16), v_m[:, :TOK].astype(bf16), weights[0]
+        )
+        self_b, mut_b = gather(
+            jnp.where(low, swap(v_own), v_s).astype(bf16),
+            swap(v_m)[:, :TOK].astype(bf16),
+            weights[1],
+        )
         return merge(mut_a, mut_b), merge(self_a, self_b)
 
     scores, weights, mutual, selfish = {}, {}, [], []
@@ -134,7 +157,7 @@
         if step < pairs:
             scores[step] = scores_of(step)
         if 0 <= step - 1 < pairs:
-            weights[step - 1] = [soften(one) for one in scores.pop(step - 1)]
+            weights[step - 1] = [soften_both(one) for one in scores.pop(step - 1)]
         if step >= 2:
             first, second = mixed(step - 2, weights.pop(step - 2))
             mutual.append(first)
@@ -265,14 +288,12 @@
         pl.semaphore_signal(
             barrier, inc=1, device_id=device, device_id_type=pl.DeviceIdType.MESH
         )
-    pl.semaphore_wait(barrier, len(known))
-
-    copy(0, 0).start()
     wk[...] = jnp.zeros_like(wk)
     raw = (w_mut, w_slf, w_prj, w_gte, w_upp, w_dwn)
     ready = (wq, wk, wv, wpm, wps, wgu, wd)
     arrange_weights(0, *raw, *ready)
-    for c in range(1, chunks):
+    pl.semaphore_wait(barrier, len(known))
+    for c in range(chunks):
         copy(0, c).start()
     arrange_weights(1, *raw, *ready)
 

time: 39.3 us -> 39.5 us (level)
  no operation moved by 1% of the time
where the time goes in v3:
time: 39.5 us; the launch traced here: 39.4 us
  Pallas kernels  36.4 us (92%)
  local copies, waits for them, and re-layouts  2.71 us (7%)
    pallas_call x1, Pallas kernels, on_device(): pl.pallas_call(both_layers, in_specs=[in_vmem] * 7, out_specs=in_vmem, ou...  36.4 us
    unnamed x13, local copies, waits for them, and re-layouts  1.54 us
    broadcast_in_dim x1, local copies, waits for them, and re-layouts, on_device(): return jnp.roll(result, half, axis=1).transpose(2, 0, 1)[None]  1.17 us

profile of v3, /device:TPU:0, one launch (start us, length us, event | category | flops | bytes accessed | tf_op | source)
XLA Modules:
  0.0 39.4 jit_solution(7403651320320473415)
XLA Ops:
  0.0 0.0 copy-start.5
  0.0 0.0 copy-start.4
  0.0 0.0 copy-start.3
  0.0 0.0 copy-start.2
  0.0 0.0 copy-start.1
  0.0 0.0 copy-start
  0.0 1.5 %copy.8 = bf16[1,120,8,256]{1,3,2,0:T(8,128)(2,1)S(1)} copy(bf16[1,120,8,256]{3,2,1,0:T(8,128)(2,1)} %param.7) | data formatting | bytes 983040 | tf_op args[0]
  1.5 0.0 copy-done.5
  1.5 0.0 copy-done.4
  1.6 0.0 copy-done.3
  1.6 0.0 copy-done.2
  1.6 0.0 copy-done.1
  1.6 0.0 copy-done
  1.6 36.4 %shard_map.73 = bf16[8,256,120]{2,1,0:T(8,128)(2,1)S(1)} custom-call(bf16[8,256,120]{2,1,0:T(8,128)(2,1)S(1)} %bitcast.9, bf16[2,120,360]{2,1,0:T(8,128)(2,1)S(1)} %copy-done, bf16[2,120,360]{2,1,0:T(8,128)(2,1)S(1)} %copy-done.1, bf16[2,240,120]{2,1,0:T(8,128)(2,1)S(1)} %copy-done.2, bf16[2,120,240]{2,1,0:T(8,128)(2,1)S(1)} %copy-done.3, ...), custom_call_target="tpu_custom_call" | custom-call | flops 2400000000 | bytes 3000000 | tf_op jit(solution)/shard_map/pallas_call | solution.py:380
  38.0 0.2 maximum_bitcast_fusion
  38.2 1.2 %copy.9 = bf16[1,120,8,256]{3,2,1,0:T(8,128)(2,1)} copy(bf16[1,120,8,256]{1,3,2,0:T(8,128)(2,1)S(1)} %maximum_bitcast_fusion) | data formatting | bytes 983040 | tf_op jit(solution)/shard_map/broadcast_in_dim | solution.py:412
  (1 shorter events, 0.0 us)
Async XLA Ops:
  0.0 1.5 %copy-start.5 = (bf16[2,240,120]{2,1,0:T(8,128)(2,1)S(1)}, bf16[2,240,120]{2,1,0:T(8,128)(2,1)}, u32[]{:S(2)}) copy-start(bf16[2,240,120]{2,1,0:T(8,128)(2,1)} %w_dwn.1) | copy-start | bytes 345604
  0.0 1.5 %copy-start.4 = (bf16[2,120,240]{2,1,0:T(8,128)(2,1)S(1)}, bf16[2,120,240]{2,1,0:T(8,128)(2,1)}, u32[]{:S(2)}) copy-start(bf16[2,120,240]{2,1,0:T(8,128)(2,1)} %w_upp.1) | copy-start | bytes 345604
  0.0 1.6 %copy-start.3 = (bf16[2,120,240]{2,1,0:T(8,128)(2,1)S(1)}, bf16[2,120,240]{2,1,0:T(8,128)(2,1)}, u32[]{:S(2)}) copy-start(bf16[2,120,240]{2,1,0:T(8,128)(2,1)} %w_gte.1) | copy-start | bytes 345604
  0.0 1.6 %copy-start.2 = (bf16[2,240,120]{2,1,0:T(8,128)(2,1)S(1)}, bf16[2,240,120]{2,1,0:T(8,128)(2,1)}, u32[]{:S(2)}) copy-start(bf16[2,240,120]{2,1,0:T(8,128)(2,1)} %w_prj.1) | copy-start | bytes 345604
  0.0 1.6 %copy-start.1 = (bf16[2,120,360]{2,1,0:T(8,128)(2,1)S(1)}, bf16[2,120,360]{2,1,0:T(8,128)(2,1)}, u32[]{:S(2)}) copy-start(bf16[2,120,360]{2,1,0:T(8,128)(2,1)} %w_slf.1) | copy-start | bytes 518404
  0.0 1.6 %copy-start = (bf16[2,120,360]{2,1,0:T(8,128)(2,1)S(1)}, bf16[2,120,360]{2,1,0:T(8,128)(2,1)}, u32[]{:S(2)}) copy-start(bf16[2,120,360]{2,1,0:T(8,128)(2,1)} %w_mut.1) | copy-start | bytes 518404

commit v4 on v3

--- a/solution.py
+++ b/solution.py
@@ -242,12 +242,14 @@
             device_id_type=pl.DeviceIdType.MESH,
         )
 
+    ahead = 1 - 2 * side
+
     def copy(group, c):
         source, target, device = (
             (x_ref.at[:, place(c, 1 - side), :], partner.at[:, span(c), :], at(0, 1 - side, 0)),
-            (upper.at[1, :, span(c), :], halves.at[1, :, span(c), :], at(0, side, -1)),
-            (lower.at[0, :, span(c), :], halves.at[2, :, span(c), :], at(-1, side, 0)),
-            (upper.at[0, :, span(c), :], halves.at[3, :, span(c), :], at(-1, side, -1)),
+            (upper.at[0, :, span(c), :], halves.at[1, :, span(c), :], at(0, side, -1)),
+            (lower.at[1, :, span(c), :], halves.at[2, :, span(c), :], at(ahead, side, 0)),
+            (upper.at[1, :, span(c), :], halves.at[3, :, span(c), :], at(ahead, side, -1)),
         )[group]
         return remote(source, target, send.at[group, c], recv.at[group, c], device)
 
@@ -255,8 +257,8 @@
         source, device = (
             (lower.at[1], at(0, 1 - side, 0)),
             (upper.at[1], at(0, 1 - side, -1)),
-            (lower.at[0], at(-1, 1 - side, 0)),
-            (upper.at[0], at(-1, 1 - side, -1)),
+            (lower.at[0], at(-ahead, 1 - side, 0)),
+            (upper.at[0], at(-ahead, 1 - side, -1)),
         )[group]
         return remote(
             source.at[:, pl.ds(0, SLACK), :],
@@ -266,14 +268,17 @@
             device,
         )
 
-    def give_back(kind, c, origin):
-        frame, part = kind // 2, kind % 2
-        device = at(1 - frame, frame, part)
+    def give_back(kind, c):
+        frame, part, device = (
+            (1, 0, at(-ahead, 1 - side, 0)),
+            (1, 1, at(-ahead, 1 - side, 1)),
+            (0, 1, at(0, side, 1)),
+        )[kind]
         return remote(
-            result.at[1 - frame, pl.ds(half * part, half), span(c), :],
-            out_ref.at[pl.ds(half * (1 - part), half), place(c, origin), :],
+            result.at[frame, pl.ds(half * part, half), span(c), :],
+            out_ref.at[pl.ds(half * (1 - part), half), place(c, side), :],
             out_send.at[kind, c],
-            out_recv.at[part, origin, c],
+            out_recv.at[kind, c],
             device,
         )
 
@@ -303,13 +308,13 @@
         own, other = layer_result(
             x_ref[:, place(c, side), :], partner[:, span(c), :], 0, *ready
         )
-        upper[side, :, span(c), :] = own[:half]
-        lower[side, :, span(c), :] = own[half:]
-        upper[1 - side, :, span(c), :] = other[:half]
-        lower[1 - side, :, span(c), :] = other[half:]
+        upper[0, :, span(c), :] = own[:half]
+        lower[0, :, span(c), :] = own[half:]
+        upper[1, :, span(c), :] = other[:half]
+        lower[1, :, span(c), :] = other[half:]
         for group in (2, 3, 1):
             copy(group, c).start()
-        halves[0, :, span(c), :] = lower[1, :, span(c), :]
+        halves[0, :, span(c), :] = own[half:]
 
         @pl.when(c == 0)
         def _():
@@ -337,35 +342,18 @@
             for group in range(4):
                 edge(group).wait_recv()
 
-        odd, even = layer_result(shifted(0, 1, c), shifted(2, 3, c), 1, *ready)
-        result[0, :, span(c), :] = odd
-        result[1, :, span(c), :] = even
-        give_back(0, c, side).start()
-        give_back(1, c, side).start()
-        give_back(3, c, side).start()
-
-        @pl.when(side == 0)
-        def _():
-            give_back(2, c, side).start()
-
-        @pl.when(side == 1)
-        def _():
-            out_ref[half:, place(c, 1), :] = odd[:half]
+        own, other = layer_result(shifted(0, 1, c), shifted(2, 3, c), 1, *ready)
+        result[0, :, span(c), :] = own
+        result[1, :, span(c), :] = other
+        out_ref[half:, place(c, side), :] = own[:half]
+        for kind in range(3):
+            give_back(kind, c).start()
 
     for c in range(chunks):
-        give_back(0, c, 0).wait_recv()
-        give_back(1, c, 0).wait_recv()
-        give_back(1, c, 1).wait_recv()
-        for kind in (0, 1, 3):
-            give_back(kind, c, side).wait_send()
+        for kind in range(3):
+            give_back(kind, c).wait()
         for group in range(4):
             copy(group, c).wait_send()
-
-    @pl.when(side == 0)
-    def _():
-        for c in range(chunks):
-            give_back(0, c, 1).wait_recv()
-            give_back(2, c, 0).wait_send()
 
     for group in range(4):
         edge(group).wait_send()
@@ -399,8 +387,8 @@
             pltpu.SemaphoreType.DMA((4, chunks)),
             pltpu.SemaphoreType.DMA((4,)),
             pltpu.SemaphoreType.DMA((4,)),
-            pltpu.SemaphoreType.DMA((4, chunks)),
-            pltpu.SemaphoreType.DMA((2, 2, chunks)),
+            pltpu.SemaphoreType.DMA((3, chunks)),
+            pltpu.SemaphoreType.DMA((3, chunks)),
         ],
         compiler_params=pltpu.CompilerParams(
             vmem_limit_bytes=48 * 1024 * 1024, collective_id=0, has_side_effects=True

time: 39.5 us -> 39.3 us (level)
  no operation moved by 1% of the time
where the time goes in v4:
time: 39.3 us; the launch traced here: 39.2 us
  Pallas kernels  36.2 us (92%)
  local copies, waits for them, and re-layouts  2.71 us (7%)
    pallas_call x1, Pallas kernels, on_device(): pl.pallas_call(both_layers, in_specs=[in_vmem] * 7, out_specs=in_vmem, ou...  36.2 us
    unnamed x13, local copies, waits for them, and re-layouts  1.54 us
    broadcast_in_dim x1, local copies, waits for them, and re-layouts, on_device(): return jnp.roll(result, half, axis=1).transpose(2, 0, 1)[None]  1.17 us

profile of v4, /device:TPU:0, one launch (start us, length us, event | category | flops | bytes accessed | tf_op | source)
XLA Modules:
  0.0 39.2 jit_solution(15794709840387258937)
XLA Ops:
  0.0 0.0 copy-start.5
  0.0 0.0 copy-start.4
  0.0 0.0 copy-start.3
  0.0 0.0 copy-start.2
  0.0 0.0 copy-start.1
  0.0 0.0 copy-start
  0.0 1.5 %copy.8 = bf16[1,120,8,256]{1,3,2,0:T(8,128)(2,1)S(1)} copy(bf16[1,120,8,256]{3,2,1,0:T(8,128)(2,1)} %param.7) | data formatting | bytes 983040 | tf_op args[0]
  1.5 0.0 copy-done.5
  1.5 0.0 copy-done.4
  1.6 0.0 copy-done.3
  1.6 0.0 copy-done.2
  1.6 0.0 copy-done.1
  1.6 0.0 copy-done
  1.6 36.2 %shard_map.73 = bf16[8,256,120]{2,1,0:T(8,128)(2,1)S(1)} custom-call(bf16[8,256,120]{2,1,0:T(8,128)(2,1)S(1)} %bitcast.9, bf16[2,120,360]{2,1,0:T(8,128)(2,1)S(1)} %copy-done, bf16[2,120,360]{2,1,0:T(8,128)(2,1)S(1)} %copy-done.1, bf16[2,240,120]{2,1,0:T(8,128)(2,1)S(1)} %copy-done.2, bf16[2,120,240]{2,1,0:T(8,128)(2,1)S(1)} %copy-done.3, ...), custom_call_target="tpu_custom_call" | custom-call | flops 2400000000 | bytes 3000000 | tf_op jit(solution)/shard_map/pallas_call | solution.py:368
  37.9 0.2 maximum_bitcast_fusion
  38.0 1.2 %copy.9 = bf16[1,120,8,256]{3,2,1,0:T(8,128)(2,1)} copy(bf16[1,120,8,256]{1,3,2,0:T(8,128)(2,1)S(1)} %maximum_bitcast_fusion) | data formatting | bytes 983040 | tf_op jit(solution)/shard_map/broadcast_in_dim | solution.py:400
  (1 shorter events, 0.0 us)
Async XLA Ops:
  0.0 1.5 %copy-start.5 = (bf16[2,240,120]{2,1,0:T(8,128)(2,1)S(1)}, bf16[2,240,120]{2,1,0:T(8,128)(2,1)}, u32[]{:S(2)}) copy-start(bf16[2,240,120]{2,1,0:T(8,128)(2,1)} %w_dwn.1) | copy-start | bytes 345604
  0.0 1.5 %copy-start.4 = (bf16[2,120,240]{2,1,0:T(8,128)(2,1)S(1)}, bf16[2,120,240]{2,1,0:T(8,128)(2,1)}, u32[]{:S(2)}) copy-start(bf16[2,120,240]{2,1,0:T(8,128)(2,1)} %w_upp.1) | copy-start | bytes 345604
  0.0 1.6 %copy-start.3 = (bf16[2,120,240]{2,1,0:T(8,128)(2,1)S(1)}, bf16[2,120,240]{2,1,0:T(8,128)(2,1)}, u32[]{:S(2)}) copy-start(bf16[2,120,240]{2,1,0:T(8,128)(2,1)} %w_gte.1) | copy-start | bytes 345604
  0.0 1.6 %copy-start.2 = (bf16[2,240,120]{2,1,0:T(8,128)(2,1)S(1)}, bf16[2,240,120]{2,1,0:T(8,128)(2,1)}, u32[]{:S(2)}) copy-start(bf16[2,240,120]{2,1,0:T(8,128)(2,1)} %w_prj.1) | copy-start | bytes 345604
  0.0 1.6 %copy-start.1 = (bf16[2,120,360]{2,1,0:T(8,128)(2,1)S(1)}, bf16[2,120,360]{2,1,0:T(8,128)(2,1)}, u32[]{:S(2)}) copy-start(bf16[2,120,360]{2,1,0:T(8,128)(2,1)} %w_slf.1) | copy-start | bytes 518404
  0.0 1.6 %copy-start = (bf16[2,120,360]{2,1,0:T(8,128)(2,1)S(1)}, bf16[2,120,360]{2,1,0:T(8,128)(2,1)}, u32[]{:S(2)}) copy-start(bf16[2,120,360]{2,1,0:T(8,128)(2,1)} %w_mut.1) | copy-start | bytes 518404

commit v5 on v4

--- a/solution.py
+++ b/solution.py
@@ -293,18 +293,23 @@
         pl.semaphore_signal(
             barrier, inc=1, device_id=device, device_id_type=pl.DeviceIdType.MESH
         )
+    pl.semaphore_wait(barrier, len(known))
+    copy(0, 0).start()
     wk[...] = jnp.zeros_like(wk)
     raw = (w_mut, w_slf, w_prj, w_gte, w_upp, w_dwn)
     ready = (wq, wk, wv, wpm, wps, wgu, wd)
     arrange_weights(0, *raw, *ready)
-    pl.semaphore_wait(barrier, len(known))
-    for c in range(chunks):
-        copy(0, c).start()
+    copy(0, 1).start()
     arrange_weights(1, *raw, *ready)
 
     @pl.loop(0, chunks)
     def _(c):
         copy(0, c).wait_recv()
+
+        @pl.when(c + 2 < chunks)
+        def _():
+            copy(0, c + 2).start()
+
         own, other = layer_result(
             x_ref[:, place(c, side), :], partner[:, span(c), :], 0, *ready
         )

time: 39.3 us -> 39.4 us (level)
  no operation moved by 1% of the time
where the time goes in v5:
time: 39.4 us; the launch traced here: 39.2 us
  Pallas kernels  36.3 us (92%)
  local copies, waits for them, and re-layouts  2.71 us (7%)
    pallas_call x1, Pallas kernels, on_device(): pl.pallas_call(both_layers, in_specs=[in_vmem] * 7, out_specs=in_vmem, ou...  36.3 us
    unnamed x13, local copies, waits for them, and re-layouts  1.54 us
    broadcast_in_dim x1, local copies, waits for them, and re-layouts, on_device(): return jnp.roll(result, half, axis=1).transpose(2, 0, 1)[None]  1.17 us

profile of v5, /device:TPU:0, one launch (start us, length us, event | category | flops | bytes accessed | tf_op | source)
XLA Modules:
  0.0 39.2 jit_solution(6569740898151483672)
XLA Ops:
  0.0 0.0 copy-start.5
  0.0 0.0 copy-start.4
  0.0 0.0 copy-start.3
  0.0 0.0 copy-start.2
  0.0 0.0 copy-start.1
  0.0 0.0 copy-start
  0.0 1.5 %copy.8 = bf16[1,120,8,256]{1,3,2,0:T(8,128)(2,1)S(1)} copy(bf16[1,120,8,256]{3,2,1,0:T(8,128)(2,1)} %param.7) | data formatting | bytes 983040 | tf_op args[0]
  1.5 0.0 copy-done.5
  1.5 0.0 copy-done.4
  1.6 0.0 copy-done.3
  1.6 0.0 copy-done.2
  1.6 0.0 copy-done.1
  1.6 0.0 copy-done
  1.6 36.3 %shard_map.73 = bf16[8,256,120]{2,1,0:T(8,128)(2,1)S(1)} custom-call(bf16[8,256,120]{2,1,0:T(8,128)(2,1)S(1)} %bitcast.9, bf16[2,120,360]{2,1,0:T(8,128)(2,1)S(1)} %copy-done, bf16[2,120,360]{2,1,0:T(8,128)(2,1)S(1)} %copy-done.1, bf16[2,240,120]{2,1,0:T(8,128)(2,1)S(1)} %copy-done.2, bf16[2,120,240]{2,1,0:T(8,128)(2,1)S(1)} %copy-done.3, ...), custom_call_target="tpu_custom_call" | custom-call | flops 2400000000 | bytes 3000000 | tf_op jit(solution)/shard_map/pallas_call | solution.py:373
  37.9 0.2 maximum_bitcast_fusion
  38.1 1.2 %copy.9 = bf16[1,120,8,256]{3,2,1,0:T(8,128)(2,1)} copy(bf16[1,120,8,256]{1,3,2,0:T(8,128)(2,1)S(1)} %maximum_bitcast_fusion) | data formatting | bytes 983040 | tf_op jit(solution)/shard_map/broadcast_in_dim | solution.py:405
  (1 shorter events, 0.0 us)
Async XLA Ops:
  0.0 1.5 %copy-start.5 = (bf16[2,240,120]{2,1,0:T(8,128)(2,1)S(1)}, bf16[2,240,120]{2,1,0:T(8,128)(2,1)}, u32[]{:S(2)}) copy-start(bf16[2,240,120]{2,1,0:T(8,128)(2,1)} %w_dwn.1) | copy-start | bytes 345604
  0.0 1.5 %copy-start.4 = (bf16[2,120,240]{2,1,0:T(8,128)(2,1)S(1)}, bf16[2,120,240]{2,1,0:T(8,128)(2,1)}, u32[]{:S(2)}) copy-start(bf16[2,120,240]{2,1,0:T(8,128)(2,1)} %w_upp.1) | copy-start | bytes 345604
  0.0 1.6 %copy-start.3 = (bf16[2,120,240]{2,1,0:T(8,128)(2,1)S(1)}, bf16[2,120,240]{2,1,0:T(8,128)(2,1)}, u32[]{:S(2)}) copy-start(bf16[2,120,240]{2,1,0:T(8,128)(2,1)} %w_gte.1) | copy-start | bytes 345604
  0.0 1.6 %copy-start.2 = (bf16[2,240,120]{2,1,0:T(8,128)(2,1)S(1)}, bf16[2,240,120]{2,1,0:T(8,128)(2,1)}, u32[]{:S(2)}) copy-start(bf16[2,240,120]{2,1,0:T(8,128)(2,1)} %w_prj.1) | copy-start | bytes 345604
  0.0 1.6 %copy-start.1 = (bf16[2,120,360]{2,1,0:T(8,128)(2,1)S(1)}, bf16[2,120,360]{2,1,0:T(8,128)(2,1)}, u32[]{:S(2)}) copy-start(bf16[2,120,360]{2,1,0:T(8,128)(2,1)} %w_slf.1) | copy-start | bytes 518404
  0.0 1.6 %copy-start = (bf16[2,120,360]{2,1,0:T(8,128)(2,1)S(1)}, bf16[2,120,360]{2,1,0:T(8,128)(2,1)}, u32[]{:S(2)}) copy-start(bf16[2,120,360]{2,1,0:T(8,128)(2,1)} %w_mut.1) | copy-start | bytes 518404

commit v6 on v5

--- a/solution.py
+++ b/solution.py
@@ -17,7 +17,7 @@
 PAIR = 2 * HEAD
 GROUP = 48
 VROWS = 3 * GROUP
-CHUNK = 32
+CHUNK = 64
 SLACK = 16
 epsilon = 1e-05
 f32 = jnp.float32

time: 39.4 us -> 43.1 us (1.094)
  Pallas kernels: 36.3 us -> 40 us
    pallas_call x1, Pallas kernels: 36.3 us -> 40 us  [on_device(): pl.pallas_call(both_layers, in_specs=[in_vmem] * 7, out_specs=in_vmem, ou...]
where the time goes in v6:
time: 43.1 us; the launch traced here: 43 us
  Pallas kernels  40 us (93%)
  local copies, waits for them, and re-layouts  2.71 us (6%)
    pallas_call x1, Pallas kernels, on_device(): pl.pallas_call(both_layers, in_specs=[in_vmem] * 7, out_specs=in_vmem, ou...  40 us
    unnamed x13, local copies, waits for them, and re-layouts  1.54 us
    broadcast_in_dim x1, local copies, waits for them, and re-layouts, on_device(): return jnp.roll(result, half, axis=1).transpose(2, 0, 1)[None]  1.17 us

profile of v6, /device:TPU:0, one launch (start us, length us, event | category | flops | bytes accessed | tf_op | source)
XLA Modules:
  0.0 43.0 jit_solution(15738827110693503123)
XLA Ops:
  0.0 0.0 copy-start.5
  0.0 0.0 copy-start.4
  0.0 0.0 copy-start.3
  0.0 0.0 copy-start.2
  0.0 0.0 copy-start.1
  0.0 0.0 copy-start
  0.0 1.5 %copy.8 = bf16[1,120,8,256]{1,3,2,0:T(8,128)(2,1)S(1)} copy(bf16[1,120,8,256]{3,2,1,0:T(8,128)(2,1)} %param.7) | data formatting | bytes 983040 | tf_op args[0]
  1.5 0.0 copy-done.5
  1.5 0.0 copy-done.4
  1.6 0.0 copy-done.3
  1.6 0.0 copy-done.2
  1.6 0.0 copy-done.1
  1.6 0.0 copy-done
  1.6 40.0 %shard_map.73 = bf16[8,256,120]{2,1,0:T(8,128)(2,1)S(1)} custom-call(bf16[8,256,120]{2,1,0:T(8,128)(2,1)S(1)} %bitcast.9, bf16[2,120,360]{2,1,0:T(8,128)(2,1)S(1)} %copy-done, bf16[2,120,360]{2,1,0:T(8,128)(2,1)S(1)} %copy-done.1, bf16[2,240,120]{2,1,0:T(8,128)(2,1)S(1)} %copy-done.2, bf16[2,120,240]{2,1,0:T(8,128)(2,1)S(1)} %copy-done.3, ...), custom_call_target="tpu_custom_call" | custom-call | flops 2400000000 | bytes 3000000 | tf_op jit(solution)/shard_map/pallas_call | solution.py:373
  41.6 0.2 maximum_bitcast_fusion
  41.8 1.2 %copy.9 = bf16[1,120,8,256]{3,2,1,0:T(8,128)(2,1)} copy(bf16[1,120,8,256]{1,3,2,0:T(8,128)(2,1)S(1)} %maximum_bitcast_fusion) | data formatting | bytes 983040 | tf_op jit(solution)/shard_map/broadcast_in_dim | solution.py:405
  (1 shorter events, 0.0 us)
Async XLA Ops:
  0.0 1.5 %copy-start.5 = (bf16[2,240,120]{2,1,0:T(8,128)(2,1)S(1)}, bf16[2,240,120]{2,1,0:T(8,128)(2,1)}, u32[]{:S(2)}) copy-start(bf16[2,240,120]{2,1,0:T(8,128)(2,1)} %w_dwn.1) | copy-start | bytes 345604
  0.0 1.5 %copy-start.4 = (bf16[2,120,240]{2,1,0:T(8,128)(2,1)S(1)}, bf16[2,120,240]{2,1,0:T(8,128)(2,1)}, u32[]{:S(2)}) copy-start(bf16[2,120,240]{2,1,0:T(8,128)(2,1)} %w_upp.1) | copy-start | bytes 345604
  0.0 1.6 %copy-start.3 = (bf16[2,120,240]{2,1,0:T(8,128)(2,1)S(1)}, bf16[2,120,240]{2,1,0:T(8,128)(2,1)}, u32[]{:S(2)}) copy-start(bf16[2,120,240]{2,1,0:T(8,128)(2,1)} %w_gte.1) | copy-start | bytes 345604
  0.0 1.6 %copy-start.2 = (bf16[2,240,120]{2,1,0:T(8,128)(2,1)S(1)}, bf16[2,240,120]{2,1,0:T(8,128)(2,1)}, u32[]{:S(2)}) copy-start(bf16[2,240,120]{2,1,0:T(8,128)(2,1)} %w_prj.1) | copy-start | bytes 345604
  0.0 1.6 %copy-start.1 = (bf16[2,120,360]{2,1,0:T(8,128)(2,1)S(1)}, bf16[2,120,360]{2,1,0:T(8,128)(2,1)}, u32[]{:S(2)}) copy-start(bf16[2,120,360]{2,1,0:T(8,128)(2,1)} %w_slf.1) | copy-start | bytes 518404
  0.0 1.6 %copy-start = (bf16[2,120,360]{2,1,0:T(8,128)(2,1)S(1)}, bf16[2,120,360]{2,1,0:T(8,128)(2,1)}, u32[]{:S(2)}) copy-start(bf16[2,120,360]{2,1,0:T(8,128)(2,1)} %w_mut.1) | copy-start | bytes 518404
